TPU v7x, 32 devices: a whole 2x2x4 slice. The times are simulated.
32 devices in a mesh: freq: 2 (over x), sx: 4 (over y, core), sy: 4 (over z).
Axes of the slice: x: 2, y: 2, z: 4, core: 2. Of those that a mesh axis runs over, the one named last changes fastest.
Arguments:
- stiffness: bfloat16 [4, 4, 3072, 3072], P('sx', 'sy', None, 'freq')
- mass_matrix: bfloat16 [4, 4, 3072, 3072], P('sx', 'sy', None, 'freq')
- omega_table: float32 [8], replicated, may hold values from 0.5 to 6
- assignment: int32 [8], P('freq'), may hold values from 0 to 7, each once
- adjoint_load: float32 [4, 4, 8, 2, 4, 768], P('sx', 'sy', 'freq'), as said below
- forward_state: bfloat16 [4, 4, 8, 2, 4, 768], P('sx', 'sy', 'freq'), may hold values from -6 to 6
- owner_index: int32 [4, 4, 4, 768], P('sx', 'sy'), may hold values from 0 to 1727
Outputs:
- adjoint: float32 [4, 4, 8, 2, 4, 768], P('sx', 'sy', 'freq')
- gradient: float32 [4, 4, 1728], P('sx', 'sy', 'freq')
- residual_level: float32 [8], P('freq')
Inputs may be any that keep to these rules, and one draw needn't show every extreme that they name: `adjoint_load`: the two copies of a face shared by neighbouring substructures are equal.
All inputs are finite; a program needn't handle non-finite values.
Results may differ from a plain program's by a relative error of at most 0.012.
Values may be sent and summed in bfloat16 or wider, within the bound.
A program may use at most 128 MiB of HBM per device.

v0:
```python
import jax
import jax.numpy as jnp
from jax import lax
from jax.sharding import PartitionSpec as P

ITERS = 4
DE_SUB = 1728


LOSS_FACTOR = 0.3


def padded(cells, sides, width):
    for axis, dim in sides:
        count = lax.axis_size(axis)
        ends = count - 1
        head = lax.slice_in_dim(cells, 0, width, axis=dim)
        tail = lax.slice_in_dim(cells, cells.shape[dim] - width, cells.shape[dim], axis=dim)
        cells = jnp.concatenate(
            [
                lax.ppermute(tail, axis, [(i, (i + 1) % count) for i in range(ends)]),
                cells,
                lax.ppermute(head, axis, [((i + 1) % count, i) for i in range(ends)]),
            ],
            axis=dim,
        )
    return cells


def face_weights():
    index_x = lax.axis_index("sx")
    size_x = lax.axis_size("sx")
    index_y = lax.axis_index("sy")
    size_y = lax.axis_size("sy")
    west_weight = jnp.where(index_x > 0, 0.5, 1.0)
    east_weight = jnp.where(index_x < size_x - 1, 0.5, 1.0)
    south_weight = jnp.where(index_y > 0, 0.5, 1.0)
    north_weight = jnp.where(index_y < size_y - 1, 0.5, 1.0)
    return jnp.stack([west_weight, east_weight, south_weight, north_weight]).astype(jnp.float32)


def assemble(local_vals):
    padded_x = padded(local_vals[:, :, 0:2].astype(jnp.bfloat16), (("sx", 2),), 1).astype(
        jnp.float32
    )
    padded_y = padded(local_vals[:, :, 2:4].astype(jnp.bfloat16), (("sy", 2),), 1).astype(
        jnp.float32
    )
    west_face = padded_x[:, :, 1] + padded_x[:, :, 0]
    east_face = padded_x[:, :, 2] + padded_x[:, :, 3]
    south_face = padded_y[:, :, 1] + padded_y[:, :, 0]
    north_face = padded_y[:, :, 2] + padded_y[:, :, 3]
    return jnp.stack([west_face, east_face, south_face, north_face], axis=2)


def mix_parts(stiff_part, mass_part, omega_sq, sign_factor):
    factor = omega_sq[:, None, None]
    real_part = (
        stiff_part[:, 0] - sign_factor * LOSS_FACTOR * stiff_part[:, 1] - factor * mass_part[:, 0]
    )
    imag_part = (
        stiff_part[:, 1] + sign_factor * LOSS_FACTOR * stiff_part[:, 0] - factor * mass_part[:, 1]
    )
    return jnp.stack([real_part, imag_part], axis=1)


def apply_rows(vector, stiff_cols, mass_cols, omega_every, sign_factor):
    face_count = vector.shape[2]
    matrix_order = face_count * vector.shape[3]
    rounded = vector.astype(jnp.bfloat16)
    pieces = lax.all_gather(rounded, "freq", axis=0, tiled=True)
    count = pieces.shape[0]
    flattened = pieces.reshape(-1, matrix_order)
    stiff_part = jnp.dot(flattened, stiff_cols, preferred_element_type=jnp.float32)
    mass_part = jnp.dot(flattened, mass_cols, preferred_element_type=jnp.float32)
    local_vals = mix_parts(
        stiff_part.reshape(count, 2, face_count, -1),
        mass_part.reshape(count, 2, face_count, -1),
        omega_every,
        sign_factor,
    )
    returned = lax.all_to_all(
        local_vals.astype(jnp.bfloat16), "freq", split_axis=0, concat_axis=3, tiled=True
    ).astype(local_vals.dtype)
    return assemble(returned)


def reduce_dots(factor_pairs, weights):
    partial_value = tuple(
        (
            jnp.sum(first_vec * second_vec * weights[None, None, :, None], axis=(1, 2, 3))
            for first_vec, second_vec in factor_pairs
        )
    )
    summed = lax.psum(partial_value, ("sx", "sy"))
    return summed


def per_freq(values):
    return values[:, None, None, None]


def face_columns(matrix, matrix_order, face_count):
    grouped = matrix.reshape(matrix_order, -1, face_count)
    return jnp.swapaxes(grouped, 1, 2).reshape(matrix_order, -1)


def body(stiffness, mass_matrix, omega_table, assignment, adjoint_load, forward_state, owner_index):
    n_freq = lax.axis_size("freq")
    slot_count = adjoint_load.shape[2]
    face_count = adjoint_load.shape[4]
    face_len = adjoint_load.shape[5]
    matrix_order = face_count * face_len
    stiff_cols = face_columns(stiffness[0, 0], matrix_order, face_count)
    mass_cols = face_columns(mass_matrix[0, 0], matrix_order, face_count)
    matches = assignment[:, None] == jnp.arange(omega_table.shape[0], dtype=jnp.int32)[None, :]
    slot_omega = jnp.sum(jnp.where(matches, omega_table[None, :], 0.0), axis=1)
    weights = face_weights()
    load_rows = adjoint_load[0, 0]
    omega_every = lax.all_gather(slot_omega, "freq", axis=0, tiled=True)

    def operate(vector, sign_factor):
        return apply_rows(vector, stiff_cols, mass_cols, omega_every, sign_factor)

    residual = load_rows
    solution = jnp.zeros_like(load_rows)
    normal_res = operate(residual, -1.0)
    direction = normal_res
    image_vec = operate(normal_res, 1.0)
    gamma_now, delta_now = reduce_dots(((normal_res, normal_res), (image_vec, image_vec)), weights)
    for iteration in range(ITERS):
        step_size = gamma_now / delta_now
        solution = solution + per_freq(step_size) * direction
        if iteration + 1 < ITERS:
            residual = residual - per_freq(step_size) * image_vec
            normal_res = operate(residual, -1.0)
            fresh = operate(normal_res, 1.0)
            gamma_next, fresh_norm, fresh_cross = reduce_dots(
                ((normal_res, normal_res), (fresh, fresh), (fresh, image_vec)), weights
            )
            beta_ratio = gamma_next / gamma_now
            direction = normal_res + per_freq(beta_ratio) * direction
            image_vec = fresh + per_freq(beta_ratio) * image_vec
            delta_now = (
                fresh_norm + 2.0 * beta_ratio * fresh_cross + beta_ratio * beta_ratio * delta_now
            )
            gamma_now = gamma_next
    cell_count = float(lax.axis_size("sx") * lax.axis_size("sy") * 2 * matrix_order)
    residual_level = jnp.log(gamma_now / cell_count)
    state_vec = forward_state[0, 0].astype(jnp.float32)
    lambda_real = solution[:, 0]
    lambda_imag = solution[:, 1]
    state_real = state_vec[:, 0]
    state_imag = state_vec[:, 1]
    product_term = (
        lambda_real * state_real
        - lambda_imag * state_imag
        - LOSS_FACTOR * (lambda_real * state_imag + lambda_imag * state_real)
    )
    dof_total = jnp.sum(product_term, axis=0)
    partial_grad = jax.ops.segment_sum(
        dof_total.reshape(-1), owner_index[0, 0].reshape(-1), num_segments=DE_SUB
    )
    grad_factor = (DE_SUB / (slot_count * n_freq * matrix_order)) ** 0.5
    gradient = lax.psum_scatter(
        -grad_factor * partial_grad, "freq", scatter_dimension=0, tiled=True
    )
    return (solution[None, None], gradient[None, None], residual_level)


def solution(mesh):
    return jax.shard_map(
        body,
        mesh=mesh,
        in_specs=(
            P("sx", "sy", None, "freq"),
            P("sx", "sy", None, "freq"),
            P(),
            P("freq"),
            P("sx", "sy", "freq", None, None, None),
            P("sx", "sy", "freq", None, None, None),
            P("sx", "sy", None, None),
        ),
        out_specs=(P("sx", "sy", "freq", None, None, None), P("sx", "sy", "freq"), P("freq")),
        check_vma=False,
    )
```

profile of v0, /device:TPU:0, one launch (start us, length us, event | category | flops | bytes accessed | tf_op | source)
XLA Modules:
  0.0 556.6 jit_solution(17382485815626452697)
XLA Ops:
  1.6 5.7 %all_gather.27 = bf16[8,2,4,768]{3,2,1,0:T(4,128)(2,1)S(1)} all-gather(bf16[4,2,4,768]{3,2,1,0:T(4,128)(2,1)S(1)} %bitcast_convert_fusion), channel_id=1, replica_groups=mesh['freq'=2,'sx'=4,'sy'=4] {'freq'}, dimensions={0}, use_global_device_ids=true | all-gather | bytes 147456 | tf_op jit(solution)/shard_map/all_gather | solution.py:71
  7.2 12.6 %copy.77 = bf16[1,1,3072,1536]{2,3,1,0:T(8,128)(2,1)} copy(bf16[1,1,3072,1536]{3,2,1,0:T(8,128)(2,1)} %param.8) | data formatting | bytes 18874368 | tf_op args[1]
  19.9 16.1 %reshape_squeeze.7 = bf16[3072,384,4]{0,2,1:T(4,128)(2,1)} reshape(bf16[1,1,3072,1536]{2,3,1,0:T(8,128)(2,1)} %copy.77) | data formatting | bytes 18874368 | tf_op jit(solution)/shard_map/reshape;squeeze | solution.py:104
  35.9 12.6 %copy.75 = bf16[1,1,3072,1536]{2,3,1,0:T(8,128)(2,1)} copy(bf16[1,1,3072,1536]{3,2,1,0:T(8,128)(2,1)} %param.7) | data formatting | bytes 18874368 | tf_op args[0]
  48.6 16.1 %reshape_squeeze.6 = bf16[3072,384,4]{0,2,1:T(4,128)(2,1)} reshape(bf16[1,1,3072,1536]{2,3,1,0:T(8,128)(2,1)} %copy.75) | data formatting | bytes 18874368 | tf_op jit(solution)/shard_map/reshape;squeeze | solution.py:104
  64.7 8.7 %fusion.14 = f32[8,2,4,384]{3,0,2,1:T(8,128)S(1)} fusion(bf16[8,2,3072,1]{2,0,3,1:T(8,128)(2,1)S(1)} %bitcast.189, bf16[3072,4,384]{0,1,2:T(4,128)(2,1)} %bitcast.173), kind=kOutput, calls=%fused_computation.15 | convolution fusion | flops 150994944 | bytes 9633792 | tf_op jit(solution)/shard_map/dot_general | solution.py:75
  75.5 8.7 %fusion.30 = f32[8,2,4,384]{3,0,2,1:T(8,128)S(1)} fusion(bf16[8,2,3072,1]{2,0,3,1:T(8,128)(2,1)S(1)} %bitcast.190, bf16[3072,4,384]{0,1,2:T(4,128)(2,1)} %bitcast.181), kind=kOutput, calls=%fused_computation.31 | convolution fusion | flops 150994944 | bytes 9633792 | tf_op jit(solution)/shard_map/dot_general | solution.py:74
  84.2 4.9 all-reduce
  103.0 4.6 collective-permute-start.2
  109.6 4.9 all_gather.29
  114.5 8.7 %fusion.12 = f32[8,2,4,384]{3,0,2,1:T(8,128)S(1)} fusion(bf16[8,2,3072,1]{2,0,3,1:T(8,128)(2,1)S(1)} %bitcast.193, bf16[3072,4,384]{0,1,2:T(4,128)(2,1)} %bitcast.174), kind=kOutput, calls=%fused_computation.13 | convolution fusion | flops 150994944 | bytes 9633792 | tf_op jit(solution)/shard_map/dot_general | solution.py:75
  123.2 8.7 %fusion.28 = f32[8,2,4,384]{3,0,2,1:T(8,128)S(1)} fusion(bf16[8,2,3072,1]{2,0,3,1:T(8,128)(2,1)S(1)} %bitcast.194, bf16[3072,4,384]{0,1,2:T(4,128)(2,1)} %bitcast.182), kind=kOutput, calls=%fused_computation.29 | convolution fusion | flops 150994944 | bytes 9633792 | tf_op jit(solution)/shard_map/dot_general | solution.py:74
  141.4 4.8 collective-permute-start.6
  152.0 32.8 %all-reduce.5 = (f32[4]{0:T(128)S(1)}, f32[4]{0:T(128)S(1)}) all-reduce(f32[4]{0:T(128)S(1)} %get-tuple-element.13, f32[4]{0:T(128)S(1)} %get-tuple-element.12), channel_id=1, replica_groups=mesh['freq'=2,'sx'=4,'sy'=4] {'sx','sy'}, use_global_device_ids=true, to_apply=%region_2.3 | all-reduce | flops 8 | bytes 64 | tf_op jit(solution)/shard_map/psum | solution.py:95
  185.0 5.0 all_gather.30
  190.0 8.7 %fusion.10 = f32[8,2,4,384]{3,0,2,1:T(8,128)S(1)} fusion(bf16[8,2,3072,1]{2,0,3,1:T(8,128)(2,1)S(1)} %bitcast.195, bf16[3072,4,384]{0,1,2:T(4,128)(2,1)} %bitcast.175), kind=kOutput, calls=%fused_computation.11 | convolution fusion | flops 150994944 | bytes 9633792 | tf_op jit(solution)/shard_map/dot_general | solution.py:75
  198.6 8.7 %fusion.26 = f32[8,2,4,384]{3,0,2,1:T(8,128)S(1)} fusion(bf16[8,2,3072,1]{2,0,3,1:T(8,128)(2,1)S(1)} %bitcast.196, bf16[3072,4,384]{0,1,2:T(4,128)(2,1)} %bitcast.183), kind=kOutput, calls=%fused_computation.27 | convolution fusion | flops 150994944 | bytes 9633792 | tf_op jit(solution)/shard_map/dot_general | solution.py:74
  207.4 6.4 %all_to_all.32 = bf16[8,2,4,384]{3,2,1,0:T(4,128)(2,1)S(1)} all-to-all(bf16[8,2,4,384]{3,2,1,0:T(4,128)(2,1)S(1)} %copy.85), channel_id=1, replica_groups=mesh['freq'=2,'sx'=4,'sy'=4] {'freq'}, dimensions={0} | all-to-all | bytes 98304 | tf_op jit(solution)/shard_map/all_to_all | solution.py:82
  215.3 4.5 collective-permute-start.10
  225.3 5.2 all_gather.31
  230.5 8.7 %fusion.8 = f32[8,2,4,384]{3,0,2,1:T(8,128)S(1)} fusion(bf16[8,2,3072,1]{2,0,3,1:T(8,128)(2,1)S(1)} %bitcast.197, bf16[3072,4,384]{0,1,2:T(4,128)(2,1)} %bitcast.176), kind=kOutput, calls=%fused_computation.9 | convolution fusion | flops 150994944 | bytes 9633792 | tf_op jit(solution)/shard_map/dot_general | solution.py:75
  239.2 8.7 %fusion.24 = f32[8,2,4,384]{3,0,2,1:T(8,128)S(1)} fusion(bf16[8,2,3072,1]{2,0,3,1:T(8,128)(2,1)S(1)} %bitcast.198, bf16[3072,4,384]{0,1,2:T(4,128)(2,1)} %bitcast.184), kind=kOutput, calls=%fused_computation.25 | convolution fusion | flops 150994944 | bytes 9633792 | tf_op jit(solution)/shard_map/dot_general | solution.py:74
  248.0 6.4 %all_to_all.33 = bf16[8,2,4,384]{3,2,1,0:T(4,128)(2,1)S(1)} all-to-all(bf16[8,2,4,384]{3,2,1,0:T(4,128)(2,1)S(1)} %copy.88), channel_id=1, replica_groups=mesh['freq'=2,'sx'=4,'sy'=4] {'freq'}, dimensions={0} | all-to-all | bytes 98304 | tf_op jit(solution)/shard_map/all_to_all | solution.py:82
  255.9 4.5 collective-permute-start.14
  266.2 32.3 %all-reduce.4 = (f32[4]{0:T(128)S(1)}, f32[4]{0:T(128)S(1)}, f32[4]{0:T(128)S(1)}) all-reduce(f32[4]{0:T(128)S(1)} %get-tuple-element.11, f32[4]{0:T(128)S(1)} %get-tuple-element.8, f32[4]{0:T(128)S(1)} %get-tuple-element.7), channel_id=1, replica_groups=mesh['freq'=2,'sx'=4,'sy'=4] {'sx','sy'}, use_global_device_ids=true, to_apply=%region_6.7 | all-reduce | flops 12 | bytes 96 | tf_op jit(solution)/shard_map/psum | solution.py:95
  298.8 4.8 all_gather.32
  303.6 8.7 %fusion.6 = f32[8,2,4,384]{3,0,2,1:T(8,128)S(1)} fusion(bf16[8,2,3072,1]{2,0,3,1:T(8,128)(2,1)S(1)} %bitcast.199, bf16[3072,4,384]{0,1,2:T(4,128)(2,1)} %bitcast.177), kind=kOutput, calls=%fused_computation.7 | convolution fusion | flops 150994944 | bytes 9633792 | tf_op jit(solution)/shard_map/dot_general | solution.py:75
  312.3 8.7 %fusion.22 = f32[8,2,4,384]{3,0,2,1:T(8,128)S(1)} fusion(bf16[8,2,3072,1]{2,0,3,1:T(8,128)(2,1)S(1)} %bitcast.200, bf16[3072,4,384]{0,1,2:T(4,128)(2,1)} %bitcast.185), kind=kOutput, calls=%fused_computation.23 | convolution fusion | flops 150994944 | bytes 9633792 | tf_op jit(solution)/shard_map/dot_general | solution.py:74
  321.1 6.4 %all_to_all.34 = bf16[8,2,4,384]{3,2,1,0:T(4,128)(2,1)S(1)} all-to-all(bf16[8,2,4,384]{3,2,1,0:T(4,128)(2,1)S(1)} %copy.91), channel_id=1, replica_groups=mesh['freq'=2,'sx'=4,'sy'=4] {'freq'}, dimensions={0} | all-to-all | bytes 98304 | tf_op jit(solution)/shard_map/all_to_all | solution.py:82
  329.0 4.5 collective-permute-start.18
  339.0 5.0 all_gather.33
  344.0 8.7 %fusion.4 = f32[8,2,4,384]{3,0,2,1:T(8,128)S(1)} fusion(bf16[8,2,3072,1]{2,0,3,1:T(8,128)(2,1)S(1)} %bitcast.201, bf16[3072,4,384]{0,1,2:T(4,128)(2,1)} %bitcast.178), kind=kOutput, calls=%fused_computation.5 | convolution fusion | flops 150994944 | bytes 9633792 | tf_op jit(solution)/shard_map/dot_general | solution.py:75
  352.7 8.7 %fusion.20 = f32[8,2,4,384]{3,0,2,1:T(8,128)S(1)} fusion(bf16[8,2,3072,1]{2,0,3,1:T(8,128)(2,1)S(1)} %bitcast.202, bf16[3072,4,384]{0,1,2:T(4,128)(2,1)} %bitcast.186), kind=kOutput, calls=%fused_computation.21 | convolution fusion | flops 150994944 | bytes 9633792 | tf_op jit(solution)/shard_map/dot_general | solution.py:74
  361.5 6.4 %all_to_all.35 = bf16[8,2,4,384]{3,2,1,0:T(4,128)(2,1)S(1)} all-to-all(bf16[8,2,4,384]{3,2,1,0:T(4,128)(2,1)S(1)} %copy.94), channel_id=1, replica_groups=mesh['freq'=2,'sx'=4,'sy'=4] {'freq'}, dimensions={0} | all-to-all | bytes 98304 | tf_op jit(solution)/shard_map/all_to_all | solution.py:82
  369.4 4.5 collective-permute-start.22
  380.5 34.6 %all-reduce.3 = (f32[4]{0:T(128)S(1)}, f32[4]{0:T(128)S(1)}, f32[4]{0:T(128)S(1)}) all-reduce(f32[4]{0:T(128)S(1)} %get-tuple-element.10, f32[4]{0:T(128)S(1)} %get-tuple-element.6, f32[4]{0:T(128)S(1)} %get-tuple-element.5), channel_id=1, replica_groups=mesh['freq'=2,'sx'=4,'sy'=4] {'sx','sy'}, use_global_device_ids=true, to_apply=%region_12.13 | all-reduce | flops 12 | bytes 96 | tf_op jit(solution)/shard_map/psum | solution.py:95
  415.2 5.2 all_gather.34
  420.5 8.7 %fusion.2 = f32[8,2,4,384]{3,0,2,1:T(8,128)S(1)} fusion(bf16[8,2,3072,1]{2,0,3,1:T(8,128)(2,1)S(1)} %bitcast.203, bf16[3072,4,384]{0,1,2:T(4,128)(2,1)} %bitcast.179), kind=kOutput, calls=%fused_computation.3 | convolution fusion | flops 150994944 | bytes 9633792 | tf_op jit(solution)/shard_map/dot_general | solution.py:75
  429.2 8.7 %fusion.18 = f32[8,2,4,384]{3,0,2,1:T(8,128)S(1)} fusion(bf16[8,2,3072,1]{2,0,3,1:T(8,128)(2,1)S(1)} %bitcast.204, bf16[3072,4,384]{0,1,2:T(4,128)(2,1)} %bitcast.187), kind=kOutput, calls=%fused_computation.19 | convolution fusion | flops 150994944 | bytes 9633792 | tf_op jit(solution)/shard_map/dot_general | solution.py:74
  438.0 6.4 %all_to_all.36 = bf16[8,2,4,384]{3,2,1,0:T(4,128)(2,1)S(1)} all-to-all(bf16[8,2,4,384]{3,2,1,0:T(4,128)(2,1)S(1)} %copy.97), channel_id=1, replica_groups=mesh['freq'=2,'sx'=4,'sy'=4] {'freq'}, dimensions={0} | all-to-all | bytes 98304 | tf_op jit(solution)/shard_map/all_to_all | solution.py:82
  445.8 4.5 collective-permute-start.26
  455.9 4.9 all_gather.35
  460.9 8.7 %fusion = f32[8,2,4,384]{3,0,2,1:T(8,128)S(1)} fusion(bf16[8,2,3072,1]{2,0,3,1:T(8,128)(2,1)S(1)} %bitcast.191, bf16[3072,4,384]{0,1,2:T(4,128)(2,1)} %bitcast.180), kind=kOutput, calls=%fused_computation.1 | convolution fusion | flops 150994944 | bytes 9633792 | tf_op jit(solution)/shard_map/dot_general | solution.py:75
  469.6 8.7 %fusion.16 = f32[8,2,4,384]{3,0,2,1:T(8,128)S(1)} fusion(bf16[8,2,3072,1]{2,0,3,1:T(8,128)(2,1)S(1)} %bitcast.192, bf16[3072,4,384]{0,1,2:T(4,128)(2,1)} %bitcast.188), kind=kOutput, calls=%fused_computation.17 | convolution fusion | flops 150994944 | bytes 9633792 | tf_op jit(solution)/shard_map/dot_general | solution.py:74
  487.7 4.5 collective-permute-start.30
  498.8 33.1 %all-reduce.2 = (f32[4]{0:T(128)S(1)}, f32[4]{0:T(128)S(1)}, f32[4]{0:T(128)S(1)}) all-reduce(f32[4]{0:T(128)S(1)} %get-tuple-element.9, f32[4]{0:T(128)S(1)} %get-tuple-element.4, f32[4]{0:T(128)S(1)} %get-tuple-element.3), channel_id=1, replica_groups=mesh['freq'=2,'sx'=4,'sy'=4] {'sx','sy'}, use_global_device_ids=true, to_apply=%region_18.19 | all-reduce | flops 12 | bytes 96 | tf_op jit(solution)/shard_map/psum | solution.py:95
  532.9 16.7 %scatter_custom_fusion = f32[1728]{0:T(1024)S(1)} fusion(s32[3072]{0:T(1024)S(1)} %reshape.442, f32[3072]{0:T(1024)S(1)} %reshape.444, f32[]{:T(128)} %constant.13.clone.1), kind=kCustom, calls=%fused_computation.196 | custom fusion | flops 3072 | bytes 6916 | tf_op jit(solution)/shard_map/scatter-add | solution.py:161
  549.6 5.0 all-reduce.1
  (199 shorter events, 88.0 us)
Async XLA Ops:
  64.7 8.7 %copy-start.4 = (f32[8]{0:T(128)S(1)}, f32[8]{0:T(128)}, u32[]{:S(2)}) copy-start(f32[8]{0:T(128)} %param.9) | copy-start | bytes 100
  64.7 8.7 %copy-start.5 = (s32[4]{0:T(128)S(1)}, s32[4]{0:T(128)}, u32[]{:S(2)}) copy-start(s32[4]{0:T(128)} %param.10) | copy-start | bytes 52
  64.7 8.9 %copy-start.3 = (u32[32]{0:T(128)S(1)}, u32[32]{0:T(128)}, u32[]{:S(2)}) copy-start(u32[32]{0:T(128)} %constant.37) | copy-start | bytes 388
  89.9 7.3 %all-to-all-start = ((bf16[8,2,4,384]{3,2,1,0:T(4,128)(2,1)}), bf16[8,2,4,384]{3,2,1,0:T(4,128)(2,1)S(1)}, u32[]{:S(2)}, u32[]{:S(2)}) async-start(bf16[8,2,4,384]{3,2,1,0:T(4,128)(2,1)} %copy.79), calls=%async_computation | async-start | bytes 98304 | tf_op jit(solution)/shard_map/all_to_all | solution.py:82
  97.4 10.3 %collective-permute-start.1 = (bf16[4,2,1,768]{3,2,1,0:T(2,128)(2,1)S(1)}, bf16[4,2,1,768]{3,2,1,0:T(2,128)(2,1)S(1)}, u32[]{:S(2)}, u32[]{:S(2)}) collective-permute-start(bf16[4,2,1,768]{3,2,1,0:T(2,128)(2,1)S(1)} %get-tuple-element.130), channel_id=1, source_target_pairs={{4,0},{8,4},{12,8},{5,1},{9,5},{13,9},{6,2},{10,6},{14,10},{7,3},{... | collective-permute-start | bytes 36872 | tf_op jit(solution)/shard_map/ppermute | solution.py:23
  98.7 9.0 %collective-permute-start = (bf16[4,2,1,768]{3,2,1,0:T(2,128)(2,1)S(1)}, bf16[4,2,1,768]{3,2,1,0:T(2,128)(2,1)S(1)}, u32[]{:S(2)}, u32[]{:S(2)}) collective-permute-start(bf16[4,2,1,768]{3,2,1,0:T(2,128)(2,1)S(1)} %get-tuple-element.127), channel_id=1, source_target_pairs={{0,4},{4,8},{8,12},{1,5},{5,9},{9,13},{2,6},{6,10},{10,14},{3,7},{... | collective-permute-start | bytes 36872 | tf_op jit(solution)/shard_map/ppermute | solution.py:21
  101.7 6.0 %collective-permute-start.3 = (bf16[4,2,1,768]{3,2,1,0:T(2,128)(2,1)S(1)}, bf16[4,2,1,768]{3,2,1,0:T(2,128)(2,1)S(1)}, u32[]{:S(2)}, u32[]{:S(2)}) collective-permute-start(bf16[4,2,1,768]{3,2,1,0:T(2,128)(2,1)S(1)} %get-tuple-element.128), channel_id=1, source_target_pairs={{1,0},{2,1},{3,2},{5,4},{6,5},{7,6},{9,8},{10,9},{11,10},{13,12},{... | collective-permute-start | bytes 36872 | tf_op jit(solution)/shard_map/ppermute | solution.py:23
  103.0 6.1 %collective-permute-start.2 = (bf16[4,2,1,768]{3,2,1,0:T(2,128)(2,1)S(1)}, bf16[4,2,1,768]{3,2,1,0:T(2,128)(2,1)S(1)}, u32[]{:S(2)}, u32[]{:S(2)}) collective-permute-start(bf16[4,2,1,768]{3,2,1,0:T(2,128)(2,1)S(1)} %get-tuple-element.129), channel_id=1, source_target_pairs={{0,1},{1,2},{2,3},{4,5},{5,6},{6,7},{8,9},{9,10},{10,11},{12,13},{... | collective-permute-start | bytes 36872 | tf_op jit(solution)/shard_map/ppermute | solution.py:21
  114.5 70.3 %copy-start = (f32[1,1,4,2,4,768]{5,4,3,2,1,0:T(4,128)S(1)}, f32[1,1,4,2,4,768]{5,4,3,2,1,0:T(4,128)}, u32[]{:S(2)}) copy-start(f32[1,1,4,2,4,768]{5,4,3,2,1,0:T(4,128)} %param.11) | copy-start | bytes 294916
  132.7 7.3 %all-to-all-start.1 = ((bf16[8,2,4,384]{3,2,1,0:T(4,128)(2,1)}), bf16[8,2,4,384]{3,2,1,0:T(4,128)(2,1)S(1)}, u32[]{:S(2)}, u32[]{:S(2)}) async-start(bf16[8,2,4,384]{3,2,1,0:T(4,128)(2,1)} %copy.82), calls=%async_computation.1 | async-start | bytes 98304 | tf_op jit(solution)/shard_map/all_to_all | solution.py:82
  140.1 10.5 %collective-permute-start.7 = (bf16[4,2,1,768]{3,2,1,0:T(2,128)(2,1)S(1)}, bf16[4,2,1,768]{3,2,1,0:T(2,128)(2,1)S(1)}, u32[]{:S(2)}, u32[]{:S(2)}) collective-permute-start(bf16[4,2,1,768]{3,2,1,0:T(2,128)(2,1)S(1)} %get-tuple-element.122), channel_id=1, source_target_pairs={{1,0},{2,1},{3,2},{5,4},{6,5},{7,6},{9,8},{10,9},{11,10},{13,12},{... | collective-permute-start | bytes 36872 | tf_op jit(solution)/shard_map/ppermute | solution.py:23
  141.4 9.2 %collective-permute-start.6 = (bf16[4,2,1,768]{3,2,1,0:T(2,128)(2,1)S(1)}, bf16[4,2,1,768]{3,2,1,0:T(2,128)(2,1)S(1)}, u32[]{:S(2)}, u32[]{:S(2)}) collective-permute-start(bf16[4,2,1,768]{3,2,1,0:T(2,128)(2,1)S(1)} %get-tuple-element.123), channel_id=1, source_target_pairs={{0,1},{1,2},{2,3},{4,5},{5,6},{6,7},{8,9},{9,10},{10,11},{12,13},{... | collective-permute-start | bytes 36872 | tf_op jit(solution)/shard_map/ppermute | solution.py:21
  146.3 4.5 collective-permute-start.5
  147.6 3.9 collective-permute-start.4
  214.0 10.2 %collective-permute-start.11 = (bf16[4,2,1,768]{3,2,1,0:T(2,128)(2,1)S(1)}, bf16[4,2,1,768]{3,2,1,0:T(2,128)(2,1)S(1)}, u32[]{:S(2)}, u32[]{:S(2)}) collective-permute-start(bf16[4,2,1,768]{3,2,1,0:T(2,128)(2,1)S(1)} %get-tuple-element.116), channel_id=1, source_target_pairs={{1,0},{2,1},{3,2},{5,4},{6,5},{7,6},{9,8},{10,9},{11,10},{13,12},{... | collective-permute-start | bytes 36872 | tf_op jit(solution)/shard_map/ppermute | solution.py:23
  215.3 9.0 %collective-permute-start.10 = (bf16[4,2,1,768]{3,2,1,0:T(2,128)(2,1)S(1)}, bf16[4,2,1,768]{3,2,1,0:T(2,128)(2,1)S(1)}, u32[]{:S(2)}, u32[]{:S(2)}) collective-permute-start(bf16[4,2,1,768]{3,2,1,0:T(2,128)(2,1)S(1)} %get-tuple-element.117), channel_id=1, source_target_pairs={{0,1},{1,2},{2,3},{4,5},{5,6},{6,7},{8,9},{9,10},{10,11},{12,13},{... | collective-permute-start | bytes 36872 | tf_op jit(solution)/shard_map/ppermute | solution.py:21
  219.9 4.5 collective-permute-start.9
  221.2 3.9 collective-permute-start.8
  254.6 10.2 %collective-permute-start.15 = (bf16[4,2,1,768]{3,2,1,0:T(2,128)(2,1)S(1)}, bf16[4,2,1,768]{3,2,1,0:T(2,128)(2,1)S(1)}, u32[]{:S(2)}, u32[]{:S(2)}) collective-permute-start(bf16[4,2,1,768]{3,2,1,0:T(2,128)(2,1)S(1)} %get-tuple-element.110), channel_id=1, source_target_pairs={{1,0},{2,1},{3,2},{5,4},{6,5},{7,6},{9,8},{10,9},{11,10},{13,12},{... | collective-permute-start | bytes 36872 | tf_op jit(solution)/shard_map/ppermute | solution.py:23
  255.9 9.0 %collective-permute-start.14 = (bf16[4,2,1,768]{3,2,1,0:T(2,128)(2,1)S(1)}, bf16[4,2,1,768]{3,2,1,0:T(2,128)(2,1)S(1)}, u32[]{:S(2)}, u32[]{:S(2)}) collective-permute-start(bf16[4,2,1,768]{3,2,1,0:T(2,128)(2,1)S(1)} %get-tuple-element.111), channel_id=1, source_target_pairs={{0,1},{1,2},{2,3},{4,5},{5,6},{6,7},{8,9},{9,10},{10,11},{12,13},{... | collective-permute-start | bytes 36872 | tf_op jit(solution)/shard_map/ppermute | solution.py:21
  260.5 4.5 collective-permute-start.13
  261.8 3.9 collective-permute-start.12
  327.7 10.2 %collective-permute-start.19 = (bf16[4,2,1,768]{3,2,1,0:T(2,128)(2,1)S(1)}, bf16[4,2,1,768]{3,2,1,0:T(2,128)(2,1)S(1)}, u32[]{:S(2)}, u32[]{:S(2)}) collective-permute-start(bf16[4,2,1,768]{3,2,1,0:T(2,128)(2,1)S(1)} %get-tuple-element.104), channel_id=1, source_target_pairs={{1,0},{2,1},{3,2},{5,4},{6,5},{7,6},{9,8},{10,9},{11,10},{13,12},{... | collective-permute-start | bytes 36872 | tf_op jit(solution)/shard_map/ppermute | solution.py:23
  329.0 9.0 %collective-permute-start.18 = (bf16[4,2,1,768]{3,2,1,0:T(2,128)(2,1)S(1)}, bf16[4,2,1,768]{3,2,1,0:T(2,128)(2,1)S(1)}, u32[]{:S(2)}, u32[]{:S(2)}) collective-permute-start(bf16[4,2,1,768]{3,2,1,0:T(2,128)(2,1)S(1)} %get-tuple-element.105), channel_id=1, source_target_pairs={{0,1},{1,2},{2,3},{4,5},{5,6},{6,7},{8,9},{9,10},{10,11},{12,13},{... | collective-permute-start | bytes 36872 | tf_op jit(solution)/shard_map/ppermute | solution.py:21
  333.6 4.5 collective-permute-start.17
  334.9 3.9 collective-permute-start.16
  368.1 11.1 %collective-permute-start.23 = (bf16[4,2,1,768]{3,2,1,0:T(2,128)(2,1)S(1)}, bf16[4,2,1,768]{3,2,1,0:T(2,128)(2,1)S(1)}, u32[]{:S(2)}, u32[]{:S(2)}) collective-permute-start(bf16[4,2,1,768]{3,2,1,0:T(2,128)(2,1)S(1)} %get-tuple-element.98), channel_id=1, source_target_pairs={{1,0},{2,1},{3,2},{5,4},{6,5},{7,6},{9,8},{10,9},{11,10},{13,12},{... | collective-permute-start | bytes 36872 | tf_op jit(solution)/shard_map/ppermute | solution.py:23
  369.4 9.8 %collective-permute-start.22 = (bf16[4,2,1,768]{3,2,1,0:T(2,128)(2,1)S(1)}, bf16[4,2,1,768]{3,2,1,0:T(2,128)(2,1)S(1)}, u32[]{:S(2)}, u32[]{:S(2)}) collective-permute-start(bf16[4,2,1,768]{3,2,1,0:T(2,128)(2,1)S(1)} %get-tuple-element.99), channel_id=1, source_target_pairs={{0,1},{1,2},{2,3},{4,5},{5,6},{6,7},{8,9},{9,10},{10,11},{12,13},{... | collective-permute-start | bytes 36872 | tf_op jit(solution)/shard_map/ppermute | solution.py:21
  374.0 5.4 collective-permute-start.21
  375.3 4.7 collective-permute-start.20
  444.5 10.2 %collective-permute-start.27 = (bf16[4,2,1,768]{3,2,1,0:T(2,128)(2,1)S(1)}, bf16[4,2,1,768]{3,2,1,0:T(2,128)(2,1)S(1)}, u32[]{:S(2)}, u32[]{:S(2)}) collective-permute-start(bf16[4,2,1,768]{3,2,1,0:T(2,128)(2,1)S(1)} %get-tuple-element.92), channel_id=1, source_target_pairs={{1,0},{2,1},{3,2},{5,4},{6,5},{7,6},{9,8},{10,9},{11,10},{13,12},{... | collective-permute-start | bytes 36872 | tf_op jit(solution)/shard_map/ppermute | solution.py:23
  445.8 9.0 %collective-permute-start.26 = (bf16[4,2,1,768]{3,2,1,0:T(2,128)(2,1)S(1)}, bf16[4,2,1,768]{3,2,1,0:T(2,128)(2,1)S(1)}, u32[]{:S(2)}, u32[]{:S(2)}) collective-permute-start(bf16[4,2,1,768]{3,2,1,0:T(2,128)(2,1)S(1)} %get-tuple-element.93), channel_id=1, source_target_pairs={{0,1},{1,2},{2,3},{4,5},{5,6},{6,7},{8,9},{9,10},{10,11},{12,13},{... | collective-permute-start | bytes 36872 | tf_op jit(solution)/shard_map/ppermute | solution.py:21
  450.4 4.5 collective-permute-start.25
  451.7 3.9 collective-permute-start.24
  460.8 21.4 %copy-start.1 = (bf16[1,1,4,2,4,768]{5,4,3,2,1,0:T(4,128)(2,1)S(1)}, bf16[1,1,4,2,4,768]{5,4,3,2,1,0:T(4,128)(2,1)}, u32[]{:S(2)}) copy-start(bf16[1,1,4,2,4,768]{5,4,3,2,1,0:T(4,128)(2,1)} %param.12) | copy-start | bytes 147460
  460.8 21.4 %copy-start.2 = (s32[1,1,4,768]{3,2,1,0:T(4,128)S(1)}, s32[1,1,4,768]{3,2,1,0:T(4,128)}, u32[]{:S(2)}) copy-start(s32[1,1,4,768]{3,2,1,0:T(4,128)} %param.13) | copy-start | bytes 36868
  479.0 7.3 %all-to-all-start.7 = ((bf16[8,2,4,384]{3,2,1,0:T(4,128)(2,1)}), bf16[8,2,4,384]{3,2,1,0:T(4,128)(2,1)S(1)}, u32[]{:S(2)}, u32[]{:S(2)}) async-start(bf16[8,2,4,384]{3,2,1,0:T(4,128)(2,1)} %copy.100), calls=%async_computation.7 | async-start | bytes 98304 | tf_op jit(solution)/shard_map/all_to_all | solution.py:82
  486.4 10.9 %collective-permute-start.31 = (bf16[4,2,1,768]{3,2,1,0:T(2,128)(2,1)S(1)}, bf16[4,2,1,768]{3,2,1,0:T(2,128)(2,1)S(1)}, u32[]{:S(2)}, u32[]{:S(2)}) collective-permute-start(bf16[4,2,1,768]{3,2,1,0:T(2,128)(2,1)S(1)} %get-tuple-element.86), channel_id=1, source_target_pairs={{1,0},{2,1},{3,2},{5,4},{6,5},{7,6},{9,8},{10,9},{11,10},{13,12},{... | collective-permute-start | bytes 36872 | tf_op jit(solution)/shard_map/ppermute | solution.py:23
  487.7 9.6 %collective-permute-start.30 = (bf16[4,2,1,768]{3,2,1,0:T(2,128)(2,1)S(1)}, bf16[4,2,1,768]{3,2,1,0:T(2,128)(2,1)S(1)}, u32[]{:S(2)}, u32[]{:S(2)}) collective-permute-start(bf16[4,2,1,768]{3,2,1,0:T(2,128)(2,1)S(1)} %get-tuple-element.87), channel_id=1, source_target_pairs={{0,1},{1,2},{2,3},{4,5},{5,6},{6,7},{8,9},{9,10},{10,11},{12,13},{... | collective-permute-start | bytes 36872 | tf_op jit(solution)/shard_map/ppermute | solution.py:21
  492.3 5.2 collective-permute-start.29
  493.6 4.6 collective-permute-start.28
where the time goes:
time: 567 us; the launch traced here: 557 us
  blocking collectives  215 us (38%)
  matrix products  139 us (25%)
  starting transfers between devices  93.1 us (16%)
  local copies, waits for them, and re-layouts  63.1 us (11%)
  other arithmetic  25.5 us (4%)
  waiting for transfers between devices  17.3 us (3%)
    psum x4, blocking collectives, reduce_dots(): summed = lax.psum(partial_value, ('sx', 'sy'))  133 us
    dot_general x8, matrix products, apply_rows(): jnp.dot(flattened, mass_cols, preferred_element_type=jnp.float32)  69.5 us
    dot_general x8, matrix products, apply_rows(): jnp.dot(flattened, stiff_cols, preferred_element_type=jnp.float32)  69.4 us
    ppermute x16, starting transfers between devices, padded(): lax.ppermute(tail, axis, [(i, (i + 1) % count) for i in range(ends)])  62.5 us
    all_gather x8, blocking collectives, apply_rows(): pieces = lax.all_gather(rounded, 'freq', axis=0, tiled=True)  40.7 us
    another operation x2, local copies, waits for them, and re-layouts, face_columns(): grouped = matrix.reshape(matrix_order, -1, face_count)  32.2 us
    all_to_all x5, blocking collectives, apply_rows(): lax.all_to_all(local_vals.astype(jnp.bfloat16), 'freq', split_axis=0, con...  32 us
    unnamed x18, local copies, waits for them, and re-layouts  26.6 us
  transfers between devices with their start and end apart: 35, of which 11 were waited for; matrix products, arithmetic and copies ran while one was open for 0% of the time, Pallas kernels for 0%

commit v1 on v0

--- a/solution.py
+++ b/solution.py
@@ -1,6 +1,10 @@
+import functools
+
 import jax
 import jax.numpy as jnp
 from jax import lax
+from jax.experimental import pallas as pl
+from jax.experimental.pallas import tpu as pltpu
 from jax.sharding import PartitionSpec as P
 
 ITERS = 4
@@ -168,9 +172,451 @@
     return (solution[None, None], gradient[None, None], residual_level)
 
 
+MESH = pl.DeviceIdType.MESH
+
+
+def fused_kernel(
+    sizes, ld, st, om, own, stiff, mass, out_sol, out_grad, out_lvl,
+    stage, mats, acc, vown, vpart, fsend, frecv, state, yloc, dacc, scal, hist,
+    red_y, red_x, red_f, ldr, stb, stw, omr, omw, solr, gsend, grecv,
+    mat_sem, pro_send, pro_recv, vs_sem, vr_sem, fs_sem, fr_sem,
+    ys_sem, yr_sem, xs_sem, xr_sem, ps_sem, pr_sem, epi_send, epi_recv,
+):
+    n_x, n_y, face_len, cells, grad_factor = sizes
+    seg = face_len // 2
+    half = 2 * seg
+    blocks = seg // 128
+    f = lax.axis_index("freq")
+    ix = lax.axis_index("sx")
+    iy = lax.axis_index("sy")
+    other = 1 - f
+    N, PD, Q, W, FR, SOL = range(6)
+
+    def mat_copy(m, r):
+        src = stiff if m == 0 else mass
+        off = (r % 4) * face_len + ((f + r // 4) % 2) * seg
+        return pltpu.make_async_copy(
+            src.at[pl.ds(pl.multiple_of(off, 128), seg)], stage.at[m, r], mat_sem.at[m, r]
+        )
+
+    for r in range(8):
+        for m in range(2):
+            mat_copy(m, r).start()
+
+    state[...] = jnp.zeros_like(state)
+    dacc[...] = jnp.zeros_like(dacc)
+    hist[...] = jnp.zeros_like(hist)
+    scal[0] = jnp.full((8, 128), -1.0, jnp.float32)
+    scal[1] = jnp.zeros((8, 128), jnp.float32)
+
+    has = (ix > 0, ix < n_x - 1, iy > 0, iy < n_y - 1)
+    peer = ({"sx": ix - 1}, {"sx": ix + 1}, {"sy": iy - 1}, {"sy": iy + 1})
+    for d in range(4):
+        @pl.when(jnp.logical_not(has[d]))
+        def _(d=d):
+            frecv[:, d] = jnp.zeros_like(frecv[:, d])
+
+    barrier = pltpu.get_barrier_semaphore()
+    for d in range(1, n_x):
+        pl.semaphore_signal(barrier, inc=1, device_id={"sx": (ix + d) % n_x}, device_id_type=MESH)
+    for d in range(1, n_y):
+        pl.semaphore_signal(barrier, inc=1, device_id={"sy": (iy + d) % n_y}, device_id_type=MESH)
+    pl.semaphore_signal(barrier, inc=1, device_id={"freq": other}, device_id_type=MESH)
+    pl.semaphore_wait(barrier, n_x + n_y - 1)
+
+    def to_partner(src, dst, ssem, rsem):
+        return pltpu.make_async_remote_copy(
+            src_ref=src, dst_ref=dst, send_sem=ssem, recv_sem=rsem,
+            device_id={"freq": other}, device_id_type=MESH,
+        )
+
+    prologue = [
+        to_partner(ld, ldr, pro_send.at[0], pro_recv.at[0]),
+        to_partner(om, omr, pro_send.at[1], pro_recv.at[1]),
+        to_partner(st, stb, pro_send.at[2], pro_recv.at[2]),
+    ]
+    for copy in prologue:
+        copy.start()
+
+    row = lax.broadcasted_iota(jnp.int32, (512, 512), 0)
+    col = lax.broadcasted_iota(jnp.int32, (512, 512), 1)
+    spread = jnp.where(row == 4 * (col % 128) + col // 128, 1.0, 0.0).astype(jnp.bfloat16)
+
+    def place(r, carry):
+        rows = pl.ds(pl.multiple_of(r * seg, 128), seg)
+        for m in range(2):
+            mat_copy(m, r).wait()
+            for b in range(blocks):
+                moved = jnp.dot(
+                    stage[m, r, :, b * 512 : (b + 1) * 512], spread,
+                    preferred_element_type=jnp.float32,
+                ).astype(jnp.bfloat16)
+                for face in range(4):
+                    lo = face * seg + b * 128
+                    mats[m, rows, lo : lo + 128] = moved[:, face * 128 : (face + 1) * 128]
+        return carry
+
+    lax.fori_loop(0, 8, place, 0)
+
+    for copy in prologue:
+        copy.wait()
+    omw[...] = om[...] + omr[...]
+    stw[...] = st[...] + stb[...]
+    for face in range(4):
+        h, k = face // 2, face % 2
+        mine = pl.ds(pl.multiple_of(face * face_len + f * seg, 128), seg)
+        theirs = pl.ds(pl.multiple_of(face * face_len + other * seg, 128), seg)
+        vown[0, h, 0:16, k * seg : (k + 1) * seg] = ld[:, mine] + ldr[:, mine]
+        vpart[0, h, 0:16, k * seg : (k + 1) * seg] = ld[:, theirs] + ldr[:, theirs]
+    for h in range(2):
+        vown[0, h, 16:32] = jnp.zeros((16, half), jnp.bfloat16)
+        vpart[0, h, 16:32] = jnp.zeros((16, half), jnp.bfloat16)
+
+    def v_copy(t, h):
+        return to_partner(vown.at[t, h], vpart.at[t, h], vs_sem.at[t, h], vr_sem.at[t, h])
+
+    def face_out(t, d):
+        return pltpu.make_async_remote_copy(
+            src_ref=fsend.at[t, d], dst_ref=frecv.at[t, d ^ 1],
+            send_sem=fs_sem.at[t, d], recv_sem=fr_sem.at[t, d ^ 1],
+            device_id=peer[d], device_id_type=MESH,
+        )
+
+    def face_in(t, d):
+        return pltpu.make_async_remote_copy(
+            src_ref=fsend.at[t, d], dst_ref=frecv.at[t, d],
+            send_sem=fs_sem.at[t, d], recv_sem=fr_sem.at[t, d],
+            device_id=peer[d], device_id_type=MESH,
+        )
+
+    def send_faces(t, h):
+        for k in range(2):
+            d = 2 * h + k
+            fsend[t, d] = yloc[h, :, k * seg : (k + 1) * seg]
+
+            @pl.when(has[d])
+            def _(d=d):
+                face_out(t, d).start()
+
+    def take_faces(t, h):
+        for k in range(2):
+            d = 2 * h + k
+
+            @pl.when(has[d])
+            def _(d=d):
+                face_in(t, d).wait()
+        got = jnp.concatenate([frecv[t, 2 * h], frecv[t, 2 * h + 1]], axis=1)
+        return yloc[h] + got
+
+    def both(x):
+        return jnp.concatenate([x, x], axis=0)[:, :1]
+
+    def lanes(x):
+        x = x[0:8] + x[8:16]
+        total = x[:, 0:128]
+        for b in range(1, blocks):
+            total = total + x[:, b * 128 : (b + 1) * 128]
+        return total
+
+    def finish_adjoint(t, h):
+        u = take_faces(t, h)
+        alpha, beta = both(scal[0]), both(scal[1])
+        w = u + beta * state[W, h]
+        n = state[N, h]
+        p = n + beta * state[PD, h]
+        state[Q, h] = state[FR, h] + beta * state[Q, h]
+        state[PD, h] = p
+        state[W, h] = w
+        state[SOL, h] = state[SOL, h] + alpha * p
+        n = n - alpha * w
+        state[N, h] = n
+        return n
+
+    def finish_image(t, h):
+        fresh = take_faces(t, h)
+        state[FR, h] = fresh
+        n, q = state[N, h], state[Q, h]
+        for k in range(2):
+            weight = jnp.where(has[2 * h + k], 0.5, 1.0).astype(jnp.float32)
+            cut = slice(k * seg, (k + 1) * seg)
+            for i, (a, b) in enumerate(((n, n), (fresh, fresh), (fresh, q))):
+                part = weight * lanes(a[:, cut] * b[:, cut])
+                dacc[8 * i : 8 * i + 8] = dacc[8 * i : 8 * i + 8] + part
+        return fresh
+
+    def pass_on(t, h, value):
+        high = value.astype(jnp.bfloat16)
+        vown[t, h, 0:16] = high
+        vown[t, h, 16:32] = (value - high.astype(jnp.float32)).astype(jnp.bfloat16)
+        v_copy(t, h).start()
+
+    def ring_copies(it, buf, axis, me, count, ssem, rsem):
+        return [
+            pltpu.make_async_remote_copy(
+                src_ref=buf.at[it, me], dst_ref=buf.at[it, me],
+                send_sem=ssem.at[it, d - 1], recv_sem=rsem.at[it, d - 1],
+                device_id={axis: (me + d) % count}, device_id_type=MESH,
+            )
+            for d in range(1, count)
+        ]
+
+    def over_y(it):
+        return ring_copies(it, red_y, "sy", iy, n_y, ys_sem, yr_sem)
+
+    def over_x(it):
+        return ring_copies(it, red_x, "sx", ix, n_x, xs_sem, xr_sem)
+
+    def over_f(it):
+        return [to_partner(red_f.at[it, 0], red_f.at[it, 1], ps_sem.at[it], pr_sem.at[it])]
+
+    def reduce_start(it):
+        red_y[it, iy] = dacc[...]
+        dacc[...] = jnp.zeros_like(dacc)
+        for copy in over_y(it):
+            copy.start()
+
+    def reduce_mid(it):
+        for copy in over_y(it):
+            copy.wait()
+        total = red_y[it, 0]
+        for j in range(1, n_y):
+            total = total + red_y[it, j]
+        red_x[it, ix] = total
+        for copy in over_x(it):
+            copy.start()
+
+    def reduce_last(it):
+        for copy in over_x(it):
+            copy.wait()
+        total = red_x[it, 0]
+        for j in range(1, n_x):
+            total = total + red_x[it, j]
+        red_f[it, 0] = total
+        for copy in over_f(it):
+            copy.start()
+
+    def reduce_end(it):
+        for copy in over_f(it):
+            copy.wait()
+        total = jnp.sum(red_f[it, 0] + red_f[it, 1], axis=1, keepdims=True)
+        total = jnp.broadcast_to(total, (24, 128))
+        gamma, norm, cross = total[0:8], total[8:16], total[16:24]
+        beta = jnp.where(it > 0, gamma / hist[0], 0.0)
+        delta = norm + 2.0 * beta * cross + beta * beta * hist[1]
+        hist[0] = gamma
+        hist[1] = delta
+        scal[0] = gamma / delta
+        scal[1] = beta
+
+    def products(v, m, rows, h):
+        out = jnp.dot(
+            v, mats[m, rows * half : (rows + 1) * half, h * half : (h + 1) * half],
+            preferred_element_type=jnp.float32,
+        )
+        return out[0:16] + out[16:32]
+
+    def apply(t, carry):
+        it = t // 2
+        adjoint_step = t % 2 == 0
+        sign = (2 * (t % 2) - 1).astype(jnp.float32) * LOSS_FACTOR
+        v = vown[t, 0]
+        for h in range(2):
+            for m in range(2):
+                acc[m, h] = products(v, m, 0, h)
+
+        @pl.when(jnp.logical_and(adjoint_step, t > 0))
+        def _():
+            pass_on(t, 1, finish_image(t - 1, 1))
+            reduce_start(it - 1)
+
+        @pl.when(jnp.logical_not(adjoint_step))
+        def _():
+            pass_on(t, 1, finish_adjoint(t - 1, 1))
+
+        v = vown[t, 1]
+        for h in range(2):
+            for m in range(2):
+                acc[m, h] = acc[m, h] + products(v, m, 1, h)
+
+        @pl.when(t > 0)
+        def _():
+            for h in range(2):
+                v_copy(t, h).wait()
+
+        @pl.when(jnp.logical_and(adjoint_step, t > 0))
+        def _():
+            reduce_mid(it - 1)
+
+        omega = both(omw[...])[0:8]
+        for h in range(2):
+            stiff_part, mass_part = (
+                acc[m, h] + products(vpart[t, 0], m, 2, h) + products(vpart[t, 1], m, 3, h)
+                for m in range(2)
+            )
+            yloc[h, 0:8] = stiff_part[0:8] - sign * stiff_part[8:16] - omega * mass_part[0:8]
+            yloc[h, 8:16] = stiff_part[8:16] + sign * stiff_part[0:8] - omega * mass_part[8:16]
+            send_faces(t, h)
+            if h == 0:
+                @pl.when(jnp.logical_and(adjoint_step, t > 0))
+                def _():
+                    reduce_last(it - 1)
+
+        @pl.when(jnp.logical_and(adjoint_step, t > 0))
+        def _():
+            reduce_end(it - 1)
+
+        @pl.when(adjoint_step)
+        def _():
+            pass_on(t + 1, 0, finish_adjoint(t, 0))
+
+        @pl.when(jnp.logical_not(adjoint_step))
+        def _():
+            fresh = finish_image(t, 0)
+
+            @pl.when(t < 2 * ITERS - 1)
+            def _():
+                pass_on(t + 1, 0, fresh)
+
+        return carry
+
+    lax.fori_loop(0, 2 * ITERS, apply, 0)
+
+    finish_image(2 * ITERS - 1, 1)
+    reduce_start(ITERS - 1)
+    reduce_mid(ITERS - 1)
+    reduce_last(ITERS - 1)
+    reduce_end(ITERS - 1)
+    out_lvl[...] = jnp.log(hist[0] / cells)
+    alpha, beta = both(scal[0]), both(scal[1])
+    for h in range(2):
+        state[SOL, h] = state[SOL, h] + alpha * (state[N, h] + beta * state[PD, h])
+    sol_copy = to_partner(state.at[SOL], solr, epi_send.at[0], epi_recv.at[0])
+    sol_copy.start()
+
+    bins = jnp.zeros((16, 128), jnp.float32)
+    for face in range(4):
+        h, k = face // 2, face % 2
+        lam = state[SOL, h, :, k * seg : (k + 1) * seg]
+        mine = pl.ds(pl.multiple_of(face * face_len + f * seg, 128), seg)
+        u = stw[:, mine].astype(jnp.float32)
+        lr, li, ur, ui = lam[0:8], lam[8:16], u[0:8], u[8:16]
+        term = lr * ur - li * ui - LOSS_FACTOR * (lr * ui + li * ur)
+        dof = jnp.sum(term, axis=0, keepdims=True)
+        owner = own[face : face + 1, pl.ds(pl.multiple_of(f * seg, 128), seg)]
+        high = lax.broadcasted_iota(jnp.int32, (16, seg), 0) == owner // 128
+        low = lax.broadcasted_iota(jnp.int32, (128, seg), 0) == owner % 128
+        low = jnp.where(low, 1.0, 0.0).astype(jnp.bfloat16)
+        rest = jnp.where(high, dof, 0.0)
+        for _ in range(3):
+            piece = rest.astype(jnp.bfloat16)
+            bins = bins + lax.dot_general(
+                piece, low, (((1,), (1,)), ((), ())), preferred_element_type=jnp.float32
+            )
+            rest = rest - piece.astype(jnp.float32)
+    gsend[...] = -grad_factor * bins
+    grad_copy = to_partner(gsend, grecv, epi_send.at[1], epi_recv.at[1])
+    grad_copy.start()
+    for face in range(4):
+        h, k = face // 2, face % 2
+        mine = pl.ds(pl.multiple_of(face * face_len + f * seg, 128), seg)
+        out_sol[:, mine] = state[SOL, h, :, k * seg : (k + 1) * seg]
+    sol_copy.wait()
+    for face in range(4):
+        h, k = face // 2, face % 2
+        theirs = pl.ds(pl.multiple_of(face * face_len + other * seg, 128), seg)
+        out_sol[:, theirs] = solr[h, :, k * seg : (k + 1) * seg]
+    grad_copy.wait()
+    out_grad[...] = gsend[...] + grecv[...]
+
+
+def fused_body(n_x, n_y, stiffness, mass_matrix, omega_table, assignment, adjoint_load, forward_state, owner_index):
+    f = lax.axis_index("freq")
+    slots = adjoint_load.shape[2]
+    face_len = adjoint_load.shape[5]
+    order = 4 * face_len
+    seg = face_len // 2
+    matches = assignment[:, None] == jnp.arange(omega_table.shape[0], dtype=jnp.int32)[None, :]
+    slot_omega = jnp.sum(jnp.where(matches, omega_table[None, :], 0.0), axis=1)
+    here = lax.broadcasted_iota(jnp.int32, (1, 2, 1, 1), 1) == f
+
+    def all_rows(x):
+        x = jnp.swapaxes(x[0, 0].astype(jnp.bfloat16), 0, 1).reshape(2, 1, slots, order)
+        return jnp.where(here, x, 0).reshape(4 * slots, order)
+
+    om = jnp.where(here[0, :, :, 0], slot_omega[None, :], 0.0).reshape(2 * slots, 1)
+    om = jnp.broadcast_to(om, (2 * slots, 128))
+    f32, bf16 = jnp.float32, jnp.bfloat16
+    steps = 2 * ITERS
+    half = 2 * seg
+    dma = pltpu.SemaphoreType.DMA
+    vmem = pl.BlockSpec(memory_space=pltpu.VMEM)
+    hbm = pl.BlockSpec(memory_space=pl.ANY)
+    grad_factor = (DE_SUB / (2 * slots * order)) ** 0.5
+    sizes = (n_x, n_y, face_len, float(n_x * n_y * 2 * order), grad_factor)
+    sol, grad, level = pl.pallas_call(
+        functools.partial(fused_kernel, sizes),
+        out_shape=(
+            jax.ShapeDtypeStruct((16, order), f32),
+            jax.ShapeDtypeStruct((16, 128), f32),
+            jax.ShapeDtypeStruct((8, 128), f32),
+        ),
+        in_specs=[vmem, vmem, vmem, vmem, hbm, hbm],
+        out_specs=(vmem, vmem, vmem),
+        scratch_shapes=[
+            pltpu.VMEM((2, 8, seg, half * 2), bf16),
+            pltpu.VMEM((2, order, half * 2), bf16),
+            pltpu.VMEM((2, 2, 16, half), f32),
+            pltpu.VMEM((steps, 2, 32, half), bf16),
+            pltpu.VMEM((steps, 2, 32, half), bf16),
+            pltpu.VMEM((steps, 4, 16, seg), f32),
+            pltpu.VMEM((steps, 4, 16, seg), f32),
+            pltpu.VMEM((6, 2, 16, half), f32),
+            pltpu.VMEM((2, 16, half), f32),
+            pltpu.VMEM((24, 128), f32),
+            pltpu.VMEM((2, 8, 128), f32),
+            pltpu.VMEM((2, 8, 128), f32),
+            pltpu.VMEM((ITERS, n_y, 24, 128), f32),
+            pltpu.VMEM((ITERS, n_x, 24, 128), f32),
+            pltpu.VMEM((ITERS, 2, 24, 128), f32),
+            pltpu.VMEM((16, order), bf16),
+            pltpu.VMEM((16, order), bf16),
+            pltpu.VMEM((16, order), bf16),
+            pltpu.VMEM((8, 128), f32),
+            pltpu.VMEM((8, 128), f32),
+            pltpu.VMEM((2, 16, half), f32),
+            pltpu.VMEM((16, 128), f32),
+            pltpu.VMEM((16, 128), f32),
+            dma((2, 8)), dma((3,)), dma((3,)),
+            dma((steps, 2)), dma((steps, 2)), dma((steps, 4)), dma((steps, 4)),
+            dma((ITERS, n_y - 1)), dma((ITERS, n_y - 1)),
+            dma((ITERS, n_x - 1)), dma((ITERS, n_x - 1)),
+            dma((ITERS,)), dma((ITERS,)), dma((2,)), dma((2,)),
+        ],
+        compiler_params=pltpu.CompilerParams(
+            collective_id=0, has_side_effects=True, vmem_limit_bytes=50 * 1024 * 1024
+        ),
+    )(all_rows(adjoint_load), all_rows(forward_state), om, owner_index[0, 0],
+      stiffness[0, 0], mass_matrix[0, 0])
+    sol = sol.reshape(2, 2, slots, 4, face_len)
+    sol = lax.dynamic_index_in_dim(sol, f, axis=1, keepdims=False)
+    sol = jnp.swapaxes(sol, 0, 1)[None, None]
+    share = DE_SUB // 2
+    grad = lax.dynamic_slice_in_dim(grad.reshape(-1), f * share, share, axis=0)
+    level = lax.dynamic_slice_in_dim(level[:, 0], f * slots, slots, axis=0)
+    return sol, grad[None, None], level
+
+
+def fits(mesh):
+    return mesh.shape["freq"] == 2 and mesh.shape["sx"] > 1 and mesh.shape["sy"] > 1
+
+
 def solution(mesh):
+    if fits(mesh):
+        run = functools.partial(fused_body, mesh.shape["sx"], mesh.shape["sy"])
+    else:
+        run = body
     return jax.shard_map(
-        body,
+        run,
         mesh=mesh,
         in_specs=(
             P("sx", "sy", None, "freq"),

time: 567 us -> 107 us (0.19); the launches traced: 557 us -> 107 us
  blocking collectives: 215 us -> 0 us
  matrix products: 139 us -> 0 us
  Pallas kernels: 0 us -> 100 us
  starting transfers between devices: 93.1 us -> 0 us
  local copies, waits for them, and re-layouts: 63.1 us -> 4.07 us
  other arithmetic: 25.5 us -> 1.93 us
  waiting for transfers between devices: 17.3 us -> 0 us
    dot_general x16 -> x0, matrix products: 139 us -> none  [the longest x8 69.5 us: apply_rows(): jnp.dot(flattened, mass_cols, preferred_element_type=jnp.float32)]
    psum x4 -> x0, blocking collectives: 133 us -> none  [reduce_dots(): summed = lax.psum(partial_value, ('sx', 'sy'))]
    pallas_call x0 -> x1, Pallas kernels: none -> 100 us  [fused_body(): pl.pallas_call(functools.partial(fused_kernel, sizes), out_shape=(jax.Sha...]
    ppermute x32 -> x0, starting transfers between devices: 83.2 us -> none  [the longest x16 62.5 us: padded(): lax.ppermute(tail, axis, [(i, (i + 1) % count) for i in range(ends)])]
    all_gather x8 -> x0, blocking collectives: 40.7 us -> none  [apply_rows(): pieces = lax.all_gather(rounded, 'freq', axis=0, tiled=True)]
    another operation x11 -> x0, local copies, waits for them, and re-layouts: 34.2 us -> none  [the longest x2 32.2 us: face_columns(): grouped = matrix.reshape(matrix_order, -1, face_count)]
    all_to_all x5 -> x0, blocking collectives: 32 us -> none  [apply_rows(): lax.all_to_all(local_vals.astype(jnp.bfloat16), 'freq', split_axis=0, con...]
    unnamed x18 -> x2, local copies, waits for them, and re-layouts: 26.6 us -> 0.71 us
  transfers between devices with their start and end apart: 35 -> 0, of which waited for: 11 -> 0; matrix products, arithmetic and copies ran while one was open for 0% -> 0% of each run, Pallas kernels for 0% -> 0%
where the time goes in v1:
time: 107 us
  Pallas kernels  100 us (93%)
  local copies, waits for them, and re-layouts  4.07 us (4%)
  other arithmetic  1.93 us (2%)
    pallas_call x1, Pallas kernels, fused_body(): pl.pallas_call(functools.partial(fused_kernel, sizes), out_shape=(jax.Sha...  100 us

profile of v1, /device:TPU:0, one launch (start us, length us, event | category | flops | bytes accessed | tf_op | source)
XLA Modules:
  0.0 107.0 jit_solution(6773049204327010278)
XLA Ops:
  0.6 0.1 broadcast_in_dim.88
  0.7 0.1 broadcast_in_dim.89
  0.8 0.9 convert_bitcast_fusion
  1.9 0.8 broadcast_in_dim.95
  2.8 0.1 broadcast_select_fusion
  2.9 0.9 select_reduce_fusion
  3.7 0.1 broadcast_select_fusion.2
  3.8 0.1 select_n.38
  3.9 0.1 broadcast_in_dim.103.om
  4.0 0.0 copy-start
  4.0 0.7 copy-done
  4.7 100.3 %shard_map.94 = (f32[16,3072]{1,0:T(8,128)S(1)}, f32[16,128]{1,0:T(8,128)S(1)}, f32[8,128]{1,0:T(8,128)S(1)}) custom-call(bf16[16,3072]{1,0:T(8,128)(2,1)S(1)} %get-tuple-element.10.ld, bf16[16,3072]{1,0:T(8,128)(2,1)S(1)} %get-tuple-element.9.st, f32[8,128]{1,0:T(8,128)S(1)} %broadcast_in_dim.103.om, s32[4,768]{1,0:T(4,128)S(1)} %bitcast.22, ...), custom_call_target="tpu_custom_call" | custom-call | tf_op jit(solution)/shard_map/pallas_call | solution.py:556
  105.0 0.1 dynamic_slice.13
  105.0 0.6 broadcast_in_dim.105
  105.6 0.6 dynamic-slice_reduce_fusion
  106.3 0.1 reshape.52
  106.4 0.7 copy_bitcast_fusion
  (8 shorter events, 0.2 us)
Async XLA Ops:
  4.0 0.7 copy-start

commit v2 on v1

--- a/solution.py
+++ b/solution.py
@@ -177,10 +177,10 @@
 
 def fused_kernel(
     sizes, ld, st, om, own, stiff, mass, out_sol, out_grad, out_lvl,
-    stage, mats, acc, vown, vpart, fsend, frecv, state, yloc, dacc, scal, hist,
-    red_y, red_x, red_f, ldr, stb, stw, omr, omw, solr, gsend, grecv,
+    stage, mats, acc, vbuf, ysend, yrecv, frecv, state, dacc, scal, hist,
+    red_y, red_x, ldr, stb, stw, omr, omw,
     mat_sem, pro_send, pro_recv, vs_sem, vr_sem, fs_sem, fr_sem,
-    ys_sem, yr_sem, xs_sem, xr_sem, ps_sem, pr_sem, epi_send, epi_recv,
+    ys_sem, yr_sem, xs_sem, xr_sem,
 ):
     n_x, n_y, face_len, cells, grad_factor = sizes
     seg = face_len // 2
@@ -194,7 +194,7 @@
 
     def mat_copy(m, r):
         src = stiff if m == 0 else mass
-        off = (r % 4) * face_len + ((f + r // 4) % 2) * seg
+        off = (2 * (r // 4) + r % 2) * face_len + ((f + r // 2) % 2) * seg
         return pltpu.make_async_copy(
             src.at[pl.ds(pl.multiple_of(off, 128), seg)], stage.at[m, r], mat_sem.at[m, r]
         )
@@ -214,15 +214,21 @@
     for d in range(4):
         @pl.when(jnp.logical_not(has[d]))
         def _(d=d):
-            frecv[:, d] = jnp.zeros_like(frecv[:, d])
+            frecv[:, :, d] = jnp.zeros_like(frecv[:, :, d])
 
     barrier = pltpu.get_barrier_semaphore()
-    for d in range(1, n_x):
-        pl.semaphore_signal(barrier, inc=1, device_id={"sx": (ix + d) % n_x}, device_id_type=MESH)
-    for d in range(1, n_y):
-        pl.semaphore_signal(barrier, inc=1, device_id={"sy": (iy + d) % n_y}, device_id_type=MESH)
+    for side in range(2):
+        where = {"freq": (f + side) % 2}
+        for d in range(1, n_x):
+            pl.semaphore_signal(
+                barrier, inc=1, device_id={"sx": (ix + d) % n_x, **where}, device_id_type=MESH
+            )
+        for d in range(1, n_y):
+            pl.semaphore_signal(
+                barrier, inc=1, device_id={"sy": (iy + d) % n_y, **where}, device_id_type=MESH
+            )
     pl.semaphore_signal(barrier, inc=1, device_id={"freq": other}, device_id_type=MESH)
-    pl.semaphore_wait(barrier, n_x + n_y - 1)
+    pl.semaphore_wait(barrier, 2 * (n_x + n_y - 2) + 1)
 
     def to_partner(src, dst, ssem, rsem):
         return pltpu.make_async_remote_copy(
@@ -262,51 +268,48 @@
         copy.wait()
     omw[...] = om[...] + omr[...]
     stw[...] = st[...] + stb[...]
-    for face in range(4):
-        h, k = face // 2, face % 2
-        mine = pl.ds(pl.multiple_of(face * face_len + f * seg, 128), seg)
-        theirs = pl.ds(pl.multiple_of(face * face_len + other * seg, 128), seg)
-        vown[0, h, 0:16, k * seg : (k + 1) * seg] = ld[:, mine] + ldr[:, mine]
-        vpart[0, h, 0:16, k * seg : (k + 1) * seg] = ld[:, theirs] + ldr[:, theirs]
+    def pieces(h):
+        for j in range(4):
+            side, face = j // 2, 2 * h + j % 2
+            here = ((f + side) % 2) * seg
+            at = pl.ds(pl.multiple_of(face * face_len + here, 128), seg)
+            yield face, here, at, slice(j * seg, (j + 1) * seg)
+
     for h in range(2):
-        vown[0, h, 16:32] = jnp.zeros((16, half), jnp.bfloat16)
-        vpart[0, h, 16:32] = jnp.zeros((16, half), jnp.bfloat16)
-
-    def v_copy(t, h):
-        return to_partner(vown.at[t, h], vpart.at[t, h], vs_sem.at[t, h], vr_sem.at[t, h])
-
-    def face_out(t, d):
+        for _, _, at, cut in pieces(h):
+            vbuf[h, 0:16, cut] = ld[:, at] + ldr[:, at]
+        vbuf[h, 16:32] = jnp.zeros((16, 2 * half), jnp.bfloat16)
+
+    def y_copy(t, h):
+        return to_partner(ysend.at[t, h], yrecv.at[t, h], vs_sem.at[t, h], vr_sem.at[t, h])
+
+    def face_copy(t, side, d, land):
+        where = {"freq": (f + side) % 2} if side else {}
         return pltpu.make_async_remote_copy(
-            src_ref=fsend.at[t, d], dst_ref=frecv.at[t, d ^ 1],
-            send_sem=fs_sem.at[t, d], recv_sem=fr_sem.at[t, d ^ 1],
-            device_id=peer[d], device_id_type=MESH,
+            src_ref=ysend.at[t, d // 2, :, pl.ds((d % 2) * seg, seg)],
+            dst_ref=frecv.at[t, side, land],
+            send_sem=fs_sem.at[t, side, d], recv_sem=fr_sem.at[t, side, land],
+            device_id={**peer[d], **where}, device_id_type=MESH,
         )
 
-    def face_in(t, d):
-        return pltpu.make_async_remote_copy(
-            src_ref=fsend.at[t, d], dst_ref=frecv.at[t, d],
-            send_sem=fs_sem.at[t, d], recv_sem=fr_sem.at[t, d],
-            device_id=peer[d], device_id_type=MESH,
-        )
-
-    def send_faces(t, h):
-        for k in range(2):
-            d = 2 * h + k
-            fsend[t, d] = yloc[h, :, k * seg : (k + 1) * seg]
-
+    def send_values(t, h):
+        for d in (2 * h, 2 * h + 1):
             @pl.when(has[d])
             def _(d=d):
-                face_out(t, d).start()
-
-    def take_faces(t, h):
-        for k in range(2):
-            d = 2 * h + k
-
+                for side in range(2):
+                    face_copy(t, side, d, d ^ 1).start()
+        y_copy(t, h).start()
+
+    def take_values(t, h):
+        for d in (2 * h, 2 * h + 1):
             @pl.when(has[d])
             def _(d=d):
-                face_in(t, d).wait()
-        got = jnp.concatenate([frecv[t, 2 * h], frecv[t, 2 * h + 1]], axis=1)
-        return yloc[h] + got
+                for side in range(2):
+                    face_copy(t, side, d, d).wait()
+        y_copy(t, h).wait()
+        got = [frecv[t, j // 2, 2 * h + j % 2] for j in range(4)]
+        local = jnp.concatenate([ysend[t, h], yrecv[t, h]], axis=1)
+        return local + jnp.concatenate(got, axis=1)
 
     def both(x):
         return jnp.concatenate([x, x], axis=0)[:, :1]
@@ -319,7 +322,7 @@
         return total
 
     def finish_adjoint(t, h):
-        u = take_faces(t, h)
+        u = take_values(t, h)
         alpha, beta = both(scal[0]), both(scal[1])
         w = u + beta * state[W, h]
         n = state[N, h]
@@ -333,22 +336,20 @@
         return n
 
     def finish_image(t, h):
-        fresh = take_faces(t, h)
+        fresh = take_values(t, h)
         state[FR, h] = fresh
         n, q = state[N, h], state[Q, h]
-        for k in range(2):
-            weight = jnp.where(has[2 * h + k], 0.5, 1.0).astype(jnp.float32)
-            cut = slice(k * seg, (k + 1) * seg)
+        for face, _, _, cut in pieces(h):
+            weight = jnp.where(has[face], 0.5, 1.0).astype(jnp.float32)
             for i, (a, b) in enumerate(((n, n), (fresh, fresh), (fresh, q))):
                 part = weight * lanes(a[:, cut] * b[:, cut])
                 dacc[8 * i : 8 * i + 8] = dacc[8 * i : 8 * i + 8] + part
         return fresh
 
-    def pass_on(t, h, value):
+    def pass_on(h, value):
         high = value.astype(jnp.bfloat16)
-        vown[t, h, 0:16] = high
-        vown[t, h, 16:32] = (value - high.astype(jnp.float32)).astype(jnp.bfloat16)
-        v_copy(t, h).start()
+        vbuf[h, 0:16] = high
+        vbuf[h, 16:32] = (value - high.astype(jnp.float32)).astype(jnp.bfloat16)
 
     def ring_copies(it, buf, axis, me, count, ssem, rsem):
         return [
@@ -366,9 +367,6 @@
     def over_x(it):
         return ring_copies(it, red_x, "sx", ix, n_x, xs_sem, xr_sem)
 
-    def over_f(it):
-        return [to_partner(red_f.at[it, 0], red_f.at[it, 1], ps_sem.at[it], pr_sem.at[it])]
-
     def reduce_start(it):
         red_y[it, iy] = dacc[...]
         dacc[...] = jnp.zeros_like(dacc)
@@ -385,21 +383,13 @@
         for copy in over_x(it):
             copy.start()
 
-    def reduce_last(it):
+    def reduce_end(it):
         for copy in over_x(it):
             copy.wait()
         total = red_x[it, 0]
         for j in range(1, n_x):
             total = total + red_x[it, j]
-        red_f[it, 0] = total
-        for copy in over_f(it):
-            copy.start()
-
-    def reduce_end(it):
-        for copy in over_f(it):
-            copy.wait()
-        total = jnp.sum(red_f[it, 0] + red_f[it, 1], axis=1, keepdims=True)
-        total = jnp.broadcast_to(total, (24, 128))
+        total = jnp.broadcast_to(jnp.sum(total, axis=1, keepdims=True), (24, 128))
         gamma, norm, cross = total[0:8], total[8:16], total[16:24]
         beta = jnp.where(it > 0, gamma / hist[0], 0.0)
         delta = norm + 2.0 * beta * cross + beta * beta * hist[1]
@@ -408,9 +398,10 @@
         scal[0] = gamma / delta
         scal[1] = beta
 
-    def products(v, m, rows, h):
+    def products(m, rows, h):
         out = jnp.dot(
-            v, mats[m, rows * half : (rows + 1) * half, h * half : (h + 1) * half],
+            vbuf[rows],
+            mats[m, rows * 2 * half : (rows + 1) * 2 * half, h * half : (h + 1) * half],
             preferred_element_type=jnp.float32,
         )
         return out[0:16] + out[16:32]
@@ -418,64 +409,43 @@
     def apply(t, carry):
         it = t // 2
         adjoint_step = t % 2 == 0
+        reducing = jnp.logical_and(adjoint_step, t > 0)
         sign = (2 * (t % 2) - 1).astype(jnp.float32) * LOSS_FACTOR
-        v = vown[t, 0]
         for h in range(2):
             for m in range(2):
-                acc[m, h] = products(v, m, 0, h)
-
-        @pl.when(jnp.logical_and(adjoint_step, t > 0))
+                acc[m, h] = products(m, 0, h)
+
+        @pl.when(reducing)
         def _():
-            pass_on(t, 1, finish_image(t - 1, 1))
+            pass_on(1, finish_image(t - 1, 1))
             reduce_start(it - 1)
 
         @pl.when(jnp.logical_not(adjoint_step))
         def _():
-            pass_on(t, 1, finish_adjoint(t - 1, 1))
-
-        v = vown[t, 1]
-        for h in range(2):
-            for m in range(2):
-                acc[m, h] = acc[m, h] + products(v, m, 1, h)
-
-        @pl.when(t > 0)
-        def _():
-            for h in range(2):
-                v_copy(t, h).wait()
-
-        @pl.when(jnp.logical_and(adjoint_step, t > 0))
-        def _():
-            reduce_mid(it - 1)
+            pass_on(1, finish_adjoint(t - 1, 1))
 
         omega = both(omw[...])[0:8]
         for h in range(2):
-            stiff_part, mass_part = (
-                acc[m, h] + products(vpart[t, 0], m, 2, h) + products(vpart[t, 1], m, 3, h)
-                for m in range(2)
-            )
-            yloc[h, 0:8] = stiff_part[0:8] - sign * stiff_part[8:16] - omega * mass_part[0:8]
-            yloc[h, 8:16] = stiff_part[8:16] + sign * stiff_part[0:8] - omega * mass_part[8:16]
-            send_faces(t, h)
+            stiff_part, mass_part = (acc[m, h] + products(m, 1, h) for m in range(2))
+            ysend[t, h, 0:8] = stiff_part[0:8] - sign * stiff_part[8:16] - omega * mass_part[0:8]
+            ysend[t, h, 8:16] = stiff_part[8:16] + sign * stiff_part[0:8] - omega * mass_part[8:16]
+            send_values(t, h)
             if h == 0:
-                @pl.when(jnp.logical_and(adjoint_step, t > 0))
+                @pl.when(reducing)
                 def _():
-                    reduce_last(it - 1)
-
-        @pl.when(jnp.logical_and(adjoint_step, t > 0))
+                    reduce_mid(it - 1)
+
+        @pl.when(reducing)
         def _():
             reduce_end(it - 1)
 
         @pl.when(adjoint_step)
         def _():
-            pass_on(t + 1, 0, finish_adjoint(t, 0))
+            pass_on(0, finish_adjoint(t, 0))
 
         @pl.when(jnp.logical_not(adjoint_step))
         def _():
-            fresh = finish_image(t, 0)
-
-            @pl.when(t < 2 * ITERS - 1)
-            def _():
-                pass_on(t + 1, 0, fresh)
+            pass_on(0, finish_image(t, 0))
 
         return carry
 
@@ -484,49 +454,33 @@
     finish_image(2 * ITERS - 1, 1)
     reduce_start(ITERS - 1)
     reduce_mid(ITERS - 1)
-    reduce_last(ITERS - 1)
     reduce_end(ITERS - 1)
     out_lvl[...] = jnp.log(hist[0] / cells)
     alpha, beta = both(scal[0]), both(scal[1])
     for h in range(2):
         state[SOL, h] = state[SOL, h] + alpha * (state[N, h] + beta * state[PD, h])
-    sol_copy = to_partner(state.at[SOL], solr, epi_send.at[0], epi_recv.at[0])
-    sol_copy.start()
 
     bins = jnp.zeros((16, 128), jnp.float32)
-    for face in range(4):
-        h, k = face // 2, face % 2
-        lam = state[SOL, h, :, k * seg : (k + 1) * seg]
-        mine = pl.ds(pl.multiple_of(face * face_len + f * seg, 128), seg)
-        u = stw[:, mine].astype(jnp.float32)
-        lr, li, ur, ui = lam[0:8], lam[8:16], u[0:8], u[8:16]
-        term = lr * ur - li * ui - LOSS_FACTOR * (lr * ui + li * ur)
-        dof = jnp.sum(term, axis=0, keepdims=True)
-        owner = own[face : face + 1, pl.ds(pl.multiple_of(f * seg, 128), seg)]
-        high = lax.broadcasted_iota(jnp.int32, (16, seg), 0) == owner // 128
-        low = lax.broadcasted_iota(jnp.int32, (128, seg), 0) == owner % 128
-        low = jnp.where(low, 1.0, 0.0).astype(jnp.bfloat16)
-        rest = jnp.where(high, dof, 0.0)
-        for _ in range(3):
-            piece = rest.astype(jnp.bfloat16)
-            bins = bins + lax.dot_general(
-                piece, low, (((1,), (1,)), ((), ())), preferred_element_type=jnp.float32
-            )
-            rest = rest - piece.astype(jnp.float32)
-    gsend[...] = -grad_factor * bins
-    grad_copy = to_partner(gsend, grecv, epi_send.at[1], epi_recv.at[1])
-    grad_copy.start()
-    for face in range(4):
-        h, k = face // 2, face % 2
-        mine = pl.ds(pl.multiple_of(face * face_len + f * seg, 128), seg)
-        out_sol[:, mine] = state[SOL, h, :, k * seg : (k + 1) * seg]
-    sol_copy.wait()
-    for face in range(4):
-        h, k = face // 2, face % 2
-        theirs = pl.ds(pl.multiple_of(face * face_len + other * seg, 128), seg)
-        out_sol[:, theirs] = solr[h, :, k * seg : (k + 1) * seg]
-    grad_copy.wait()
-    out_grad[...] = gsend[...] + grecv[...]
+    for h in range(2):
+        for face, here, at, cut in pieces(h):
+            lam = state[SOL, h, :, cut]
+            out_sol[:, at] = lam
+            u = stw[:, at].astype(jnp.float32)
+            lr, li, ur, ui = lam[0:8], lam[8:16], u[0:8], u[8:16]
+            term = lr * ur - li * ui - LOSS_FACTOR * (lr * ui + li * ur)
+            dof = jnp.sum(term, axis=0, keepdims=True)
+            owner = own[face : face + 1, pl.ds(pl.multiple_of(here, 128), seg)]
+            high = lax.broadcasted_iota(jnp.int32, (16, seg), 0) == owner // 128
+            low = lax.broadcasted_iota(jnp.int32, (128, seg), 0) == owner % 128
+            low = jnp.where(low, 1.0, 0.0).astype(jnp.bfloat16)
+            rest = jnp.where(high, dof, 0.0)
+            for _ in range(3):
+                piece = rest.astype(jnp.bfloat16)
+                bins = bins + lax.dot_general(
+                    piece, low, (((1,), (1,)), ((), ())), preferred_element_type=jnp.float32
+                )
+                rest = rest - piece.astype(jnp.float32)
+    out_grad[...] = -grad_factor * bins
 
 
 def fused_body(n_x, n_y, stiffness, mass_matrix, omega_table, assignment, adjoint_load, forward_state, owner_index):
@@ -566,31 +520,25 @@
             pltpu.VMEM((2, 8, seg, half * 2), bf16),
             pltpu.VMEM((2, order, half * 2), bf16),
             pltpu.VMEM((2, 2, 16, half), f32),
-            pltpu.VMEM((steps, 2, 32, half), bf16),
-            pltpu.VMEM((steps, 2, 32, half), bf16),
-            pltpu.VMEM((steps, 4, 16, seg), f32),
-            pltpu.VMEM((steps, 4, 16, seg), f32),
-            pltpu.VMEM((6, 2, 16, half), f32),
-            pltpu.VMEM((2, 16, half), f32),
+            pltpu.VMEM((2, 32, 2 * half), bf16),
+            pltpu.VMEM((steps, 2, 16, half), f32),
+            pltpu.VMEM((steps, 2, 16, half), f32),
+            pltpu.VMEM((steps, 2, 4, 16, seg), f32),
+            pltpu.VMEM((6, 2, 16, 2 * half), f32),
             pltpu.VMEM((24, 128), f32),
             pltpu.VMEM((2, 8, 128), f32),
             pltpu.VMEM((2, 8, 128), f32),
             pltpu.VMEM((ITERS, n_y, 24, 128), f32),
             pltpu.VMEM((ITERS, n_x, 24, 128), f32),
-            pltpu.VMEM((ITERS, 2, 24, 128), f32),
             pltpu.VMEM((16, order), bf16),
             pltpu.VMEM((16, order), bf16),
             pltpu.VMEM((16, order), bf16),
             pltpu.VMEM((8, 128), f32),
             pltpu.VMEM((8, 128), f32),
-            pltpu.VMEM((2, 16, half), f32),
-            pltpu.VMEM((16, 128), f32),
-            pltpu.VMEM((16, 128), f32),
             dma((2, 8)), dma((3,)), dma((3,)),
-            dma((steps, 2)), dma((steps, 2)), dma((steps, 4)), dma((steps, 4)),
+            dma((steps, 2)), dma((steps, 2)), dma((steps, 2, 4)), dma((steps, 2, 4)),
             dma((ITERS, n_y - 1)), dma((ITERS, n_y - 1)),
             dma((ITERS, n_x - 1)), dma((ITERS, n_x - 1)),
-            dma((ITERS,)), dma((ITERS,)), dma((2,)), dma((2,)),
         ],
         compiler_params=pltpu.CompilerParams(
             collective_id=0, has_side_effects=True, vmem_limit_bytes=50 * 1024 * 1024

time: 107 us -> 96.2 us (0.90)
  Pallas kernels: 100 us -> 89.2 us
    pallas_call x1, Pallas kernels: 100 us -> 89.2 us  [fused_body(): pl.pallas_call(functools.partial(fused_kernel, sizes), out_shape=(jax.Sha...]
where the time goes in v2:
time: 96.2 us; the launch traced here: 95.9 us
  Pallas kernels  89.2 us (93%)
  local copies, waits for them, and re-layouts  4.07 us (4%)
  other arithmetic  1.93 us (2%)
    pallas_call x1, Pallas kernels, fused_body(): pl.pallas_call(functools.partial(fused_kernel, sizes), out_shape=(jax.Sha...  89.2 us

profile of v2, /device:TPU:0, one launch (start us, length us, event | category | flops | bytes accessed | tf_op | source)
XLA Modules:
  0.0 95.9 jit_solution(15499204603637036878)
XLA Ops:
  0.6 0.1 broadcast_in_dim.88
  0.7 0.1 broadcast_in_dim.89
  0.8 0.9 convert_bitcast_fusion
  1.9 0.8 broadcast_in_dim.95
  2.8 0.1 broadcast_select_fusion
  2.9 0.9 select_reduce_fusion
  3.7 0.1 broadcast_select_fusion.2
  3.8 0.1 select_n.38
  3.9 0.1 broadcast_in_dim.103.om
  4.0 0.0 copy-start
  4.0 0.7 copy-done
  4.7 89.2 %shard_map.94 = (f32[16,3072]{1,0:T(8,128)S(1)}, f32[16,128]{1,0:T(8,128)S(1)}, f32[8,128]{1,0:T(8,128)S(1)}) custom-call(bf16[16,3072]{1,0:T(8,128)(2,1)S(1)} %get-tuple-element.10.ld, bf16[16,3072]{1,0:T(8,128)(2,1)S(1)} %get-tuple-element.9.st, f32[8,128]{1,0:T(8,128)S(1)} %broadcast_in_dim.103.om, s32[4,768]{1,0:T(4,128)S(1)} %bitcast.22, ...), custom_call_target="tpu_custom_call" | custom-call | tf_op jit(solution)/shard_map/pallas_call | solution.py:510
  93.8 0.1 dynamic_slice.13
  93.9 0.6 broadcast_in_dim.105
  94.5 0.6 dynamic-slice_reduce_fusion
  95.1 0.1 reshape.52
  95.2 0.7 copy_bitcast_fusion
  (8 shorter events, 0.2 us)
Async XLA Ops:
  4.0 0.7 copy-start

commit v3 on v2

--- a/solution.py
+++ b/solution.py
@@ -173,6 +173,7 @@
 
 
 MESH = pl.DeviceIdType.MESH
+NROWS = 128
 
 
 def fused_kernel(
@@ -204,6 +205,7 @@
             mat_copy(m, r).start()
 
     state[...] = jnp.zeros_like(state)
+    vbuf[...] = jnp.zeros_like(vbuf)
     dacc[...] = jnp.zeros_like(dacc)
     hist[...] = jnp.zeros_like(hist)
     scal[0] = jnp.full((8, 128), -1.0, jnp.float32)
@@ -246,20 +248,20 @@
 
     row = lax.broadcasted_iota(jnp.int32, (512, 512), 0)
     col = lax.broadcasted_iota(jnp.int32, (512, 512), 1)
-    spread = jnp.where(row == 4 * (col % 128) + col // 128, 1.0, 0.0).astype(jnp.bfloat16)
+    spread = jnp.where(col == 4 * (row % 128) + row // 128, 1.0, 0.0).astype(jnp.bfloat16)
 
     def place(r, carry):
         rows = pl.ds(pl.multiple_of(r * seg, 128), seg)
         for m in range(2):
             mat_copy(m, r).wait()
             for b in range(blocks):
-                moved = jnp.dot(
-                    stage[m, r, :, b * 512 : (b + 1) * 512], spread,
+                moved = lax.dot_general(
+                    spread, stage[m, r, :, b * 512 : (b + 1) * 512], (((1,), (1,)), ((), ())),
                     preferred_element_type=jnp.float32,
                 ).astype(jnp.bfloat16)
                 for face in range(4):
                     lo = face * seg + b * 128
-                    mats[m, rows, lo : lo + 128] = moved[:, face * 128 : (face + 1) * 128]
+                    mats[m, lo : lo + 128, rows] = moved[face * 128 : (face + 1) * 128]
         return carry
 
     lax.fori_loop(0, 8, place, 0)
@@ -277,8 +279,9 @@
 
     for h in range(2):
         for _, _, at, cut in pieces(h):
-            vbuf[h, 0:16, cut] = ld[:, at] + ldr[:, at]
-        vbuf[h, 16:32] = jnp.zeros((16, 2 * half), jnp.bfloat16)
+            start = ld[:, at] + ldr[:, at]
+            vbuf[h, 0, 0:16, cut] = start
+            vbuf[h, 1, 32:48, cut] = start
 
     def y_copy(t, h):
         return to_partner(ysend.at[t, h], yrecv.at[t, h], vs_sem.at[t, h], vr_sem.at[t, h])
@@ -348,8 +351,10 @@
 
     def pass_on(h, value):
         high = value.astype(jnp.bfloat16)
-        vbuf[h, 0:16] = high
-        vbuf[h, 16:32] = (value - high.astype(jnp.float32)).astype(jnp.bfloat16)
+        low = (value - high.astype(jnp.float32)).astype(jnp.bfloat16)
+        for m in range(2):
+            vbuf[h, m, 32 * m : 32 * m + 16] = high
+            vbuf[h, m, 32 * m + 16 : 32 * m + 32] = low
 
     def ring_copies(it, buf, axis, me, count, ssem, rsem):
         return [
@@ -398,13 +403,16 @@
         scal[0] = gamma / delta
         scal[1] = beta
 
-    def products(m, rows, h):
-        out = jnp.dot(
-            vbuf[rows],
-            mats[m, rows * 2 * half : (rows + 1) * 2 * half, h * half : (h + 1) * half],
-            preferred_element_type=jnp.float32,
-        )
-        return out[0:16] + out[16:32]
+    def products(rows, h):
+        out = [
+            lax.dot_general(
+                mats[m, h * half : (h + 1) * half, rows * 2 * half : (rows + 1) * 2 * half],
+                vbuf[rows, m], (((1,), (1,)), ((), ())),
+                preferred_element_type=jnp.float32,
+            )
+            for m in range(2)
+        ]
+        return out[0] + out[1]
 
     def apply(t, carry):
         it = t // 2
@@ -412,8 +420,7 @@
         reducing = jnp.logical_and(adjoint_step, t > 0)
         sign = (2 * (t % 2) - 1).astype(jnp.float32) * LOSS_FACTOR
         for h in range(2):
-            for m in range(2):
-                acc[m, h] = products(m, 0, h)
+            acc[h] = products(0, h)
 
         @pl.when(reducing)
         def _():
@@ -426,7 +433,9 @@
 
         omega = both(omw[...])[0:8]
         for h in range(2):
-            stiff_part, mass_part = (acc[m, h] + products(m, 1, h) for m in range(2))
+            done = jnp.transpose(acc[h] + products(1, h))
+            stiff_part = done[0:16] + done[16:32]
+            mass_part = done[32:48] + done[48:64]
             ysend[t, h, 0:8] = stiff_part[0:8] - sign * stiff_part[8:16] - omega * mass_part[0:8]
             ysend[t, h, 8:16] = stiff_part[8:16] + sign * stiff_part[0:8] - omega * mass_part[8:16]
             send_values(t, h)
@@ -518,9 +527,9 @@
         out_specs=(vmem, vmem, vmem),
         scratch_shapes=[
             pltpu.VMEM((2, 8, seg, half * 2), bf16),
-            pltpu.VMEM((2, order, half * 2), bf16),
-            pltpu.VMEM((2, 2, 16, half), f32),
-            pltpu.VMEM((2, 32, 2 * half), bf16),
+            pltpu.VMEM((2, half * 2, order), bf16),
+            pltpu.VMEM((2, half, NROWS), f32),
+            pltpu.VMEM((2, 2, NROWS, 2 * half), bf16),
             pltpu.VMEM((steps, 2, 16, half), f32),
             pltpu.VMEM((steps, 2, 16, half), f32),
             pltpu.VMEM((steps, 2, 4, 16, seg), f32),

time: 96.2 us -> 118 us (1.23)
  Pallas kernels: 89.2 us -> 111 us
    pallas_call x1, Pallas kernels: 89.2 us -> 111 us  [fused_body(): pl.pallas_call(functools.partial(fused_kernel, sizes), out_shape=(jax.Sha...]
where the time goes in v3:
time: 118 us
  Pallas kernels  111 us (94%)
  local copies, waits for them, and re-layouts  4.07 us (3%)
  other arithmetic  1.93 us (2%)
    pallas_call x1, Pallas kernels, fused_body(): pl.pallas_call(functools.partial(fused_kernel, sizes), out_shape=(jax.Sha...  111 us

profile of v3, /device:TPU:0, one launch (start us, length us, event | category | flops | bytes accessed | tf_op | source)
XLA Modules:
  0.0 118.1 jit_solution(12174997972247339620)
XLA Ops:
  0.6 0.1 broadcast_in_dim.88
  0.7 0.1 broadcast_in_dim.89
  0.8 0.9 convert_bitcast_fusion
  1.9 0.8 broadcast_in_dim.95
  2.8 0.1 broadcast_select_fusion
  2.9 0.9 select_reduce_fusion
  3.7 0.1 broadcast_select_fusion.2
  3.8 0.1 select_n.38
  3.9 0.1 broadcast_in_dim.103.om
  4.0 0.0 copy-start
  4.0 0.7 copy-done
  4.7 111.4 %shard_map.94 = (f32[16,3072]{1,0:T(8,128)S(1)}, f32[16,128]{1,0:T(8,128)S(1)}, f32[8,128]{1,0:T(8,128)S(1)}) custom-call(bf16[16,3072]{1,0:T(8,128)(2,1)S(1)} %get-tuple-element.10.ld, bf16[16,3072]{1,0:T(8,128)(2,1)S(1)} %get-tuple-element.9.st, f32[8,128]{1,0:T(8,128)S(1)} %broadcast_in_dim.103.om, s32[4,768]{1,0:T(4,128)S(1)} %bitcast.22, ...), custom_call_target="tpu_custom_call" | custom-call | tf_op jit(solution)/shard_map/pallas_call | solution.py:519
  116.1 0.1 dynamic_slice.13
  116.2 0.6 broadcast_in_dim.105
  116.8 0.6 dynamic-slice_reduce_fusion
  117.4 0.1 reshape.52
  117.5 0.7 copy_bitcast_fusion
  (8 shorter events, 0.2 us)
Async XLA Ops:
  4.0 0.7 copy-start

commit v4 on v2

--- a/solution.py
+++ b/solution.py
@@ -176,9 +176,9 @@
 
 
 def fused_kernel(
-    sizes, ld, st, om, own, stiff, mass, out_sol, out_grad, out_lvl,
+    sizes, load, state_in, table, slot_of, own, stiff, mass, out_sol, out_grad, out_lvl,
     stage, mats, acc, vbuf, ysend, yrecv, frecv, state, dacc, scal, hist,
-    red_y, red_x, ldr, stb, stw, omr, omw,
+    red_y, red_x, ld, ldr, st, stb, om, omr, omw,
     mat_sem, pro_send, pro_recv, vs_sem, vr_sem, fs_sem, fr_sem,
     ys_sem, yr_sem, xs_sem, xr_sem,
 ):
@@ -215,6 +215,24 @@
         @pl.when(jnp.logical_not(has[d]))
         def _(d=d):
             frecv[:, :, d] = jnp.zeros_like(frecv[:, :, d])
+
+    slots = slot_of.shape[0]
+    ld[...] = jnp.zeros_like(ld)
+    st[...] = jnp.zeros_like(st)
+    line = lax.broadcasted_iota(jnp.int32, (8, 128), 0)
+    spots = jnp.zeros((8, 128), jnp.float32)
+    for s in range(slots):
+        value = jnp.float32(0.0)
+        for j in range(table.shape[0]):
+            value = value + jnp.where(slot_of[s] == j, table[j], 0.0)
+        spots = jnp.where(line == f * slots + s, value, spots)
+        for c in range(2):
+            for src, dst in ((load, ld), (state_in, st)):
+                tile = src[s, c].astype(jnp.float32)
+                for face in range(4):
+                    at = pl.ds(8 * c + f * slots + s, 1)
+                    dst[at, face * face_len : (face + 1) * face_len] = tile[face : face + 1]
+    om[...] = spots
 
     barrier = pltpu.get_barrier_semaphore()
     for side in range(2):
@@ -244,30 +262,39 @@
     for copy in prologue:
         copy.start()
 
-    row = lax.broadcasted_iota(jnp.int32, (512, 512), 0)
-    col = lax.broadcasted_iota(jnp.int32, (512, 512), 1)
-    spread = jnp.where(row == 4 * (col % 128) + col // 128, 1.0, 0.0).astype(jnp.bfloat16)
+    row = lax.broadcasted_iota(jnp.int32, (256, 256), 0)
+    col = lax.broadcasted_iota(jnp.int32, (256, 256), 1)
+    spread = [
+        jnp.where(row == 4 * (col % 64) + ((col // 64) ^ flip), 1.0, 0.0).astype(jnp.bfloat16)
+        for flip in range(2)
+    ]
+    first = lax.broadcasted_iota(jnp.int32, (seg, 128), 1) < 64
 
     def place(r, carry):
         rows = pl.ds(pl.multiple_of(r * seg, 128), seg)
         for m in range(2):
             mat_copy(m, r).wait()
             for b in range(blocks):
-                moved = jnp.dot(
-                    stage[m, r, :, b * 512 : (b + 1) * 512], spread,
-                    preferred_element_type=jnp.float32,
-                ).astype(jnp.bfloat16)
-                for face in range(4):
-                    lo = face * seg + b * 128
-                    mats[m, rows, lo : lo + 128] = moved[:, face * 128 : (face + 1) * 128]
+                lower, upper = (
+                    jnp.dot(
+                        stage[m, r, :, b * 512 + i * 256 : b * 512 + (i + 1) * 256], spread[i],
+                        preferred_element_type=jnp.float32,
+                    )
+                    for i in range(2)
+                )
+                for h in range(2):
+                    a, z = lower[:, h * 128 : (h + 1) * 128], upper[:, h * 128 : (h + 1) * 128]
+                    lo = h * half + b * 128
+                    even, odd = jnp.where(first, a, z), jnp.where(first, z, a)
+                    mats[m, rows, lo : lo + 128] = even.astype(jnp.bfloat16)
+                    mats[m, rows, lo + seg : lo + seg + 128] = odd.astype(jnp.bfloat16)
         return carry
 
     lax.fori_loop(0, 8, place, 0)
 
-    for copy in prologue:
+    for copy in prologue[:2]:
         copy.wait()
     omw[...] = om[...] + omr[...]
-    stw[...] = st[...] + stb[...]
     def pieces(h):
         for j in range(4):
             side, face = j // 2, 2 * h + j % 2
@@ -277,7 +304,7 @@
 
     for h in range(2):
         for _, _, at, cut in pieces(h):
-            vbuf[h, 0:16, cut] = ld[:, at] + ldr[:, at]
+            vbuf[h, 0:16, cut] = (ld[:, at] + ldr[:, at]).astype(jnp.bfloat16)
         vbuf[h, 16:32] = jnp.zeros((16, 2 * half), jnp.bfloat16)
 
     def y_copy(t, h):
@@ -427,8 +454,14 @@
         omega = both(omw[...])[0:8]
         for h in range(2):
             stiff_part, mass_part = (acc[m, h] + products(m, 1, h) for m in range(2))
-            ysend[t, h, 0:8] = stiff_part[0:8] - sign * stiff_part[8:16] - omega * mass_part[0:8]
-            ysend[t, h, 8:16] = stiff_part[8:16] + sign * stiff_part[0:8] - omega * mass_part[8:16]
+            real = stiff_part[0:8] - sign * stiff_part[8:16] - omega * mass_part[0:8]
+            imag = stiff_part[8:16] + sign * stiff_part[0:8] - omega * mass_part[8:16]
+            for c, values in enumerate((real, imag)):
+                ysend[t, h, 8 * c : 8 * c + 8, 0:seg] = values[:, 0:seg]
+                for b in range(blocks):
+                    lo = seg + b * 128
+                    turned = pltpu.roll(values[:, lo : lo + 128], 64, 1)
+                    ysend[t, h, 8 * c : 8 * c + 8, lo : lo + 128] = turned
             send_values(t, h)
             if h == 0:
                 @pl.when(reducing)
@@ -460,12 +493,13 @@
     for h in range(2):
         state[SOL, h] = state[SOL, h] + alpha * (state[N, h] + beta * state[PD, h])
 
+    prologue[2].wait()
     bins = jnp.zeros((16, 128), jnp.float32)
     for h in range(2):
         for face, here, at, cut in pieces(h):
             lam = state[SOL, h, :, cut]
             out_sol[:, at] = lam
-            u = stw[:, at].astype(jnp.float32)
+            u = st[:, at] + stb[:, at]
             lr, li, ur, ui = lam[0:8], lam[8:16], u[0:8], u[8:16]
             term = lr * ur - li * ui - LOSS_FACTOR * (lr * ui + li * ur)
             dof = jnp.sum(term, axis=0, keepdims=True)
@@ -489,22 +523,13 @@
     face_len = adjoint_load.shape[5]
     order = 4 * face_len
     seg = face_len // 2
-    matches = assignment[:, None] == jnp.arange(omega_table.shape[0], dtype=jnp.int32)[None, :]
-    slot_omega = jnp.sum(jnp.where(matches, omega_table[None, :], 0.0), axis=1)
-    here = lax.broadcasted_iota(jnp.int32, (1, 2, 1, 1), 1) == f
-
-    def all_rows(x):
-        x = jnp.swapaxes(x[0, 0].astype(jnp.bfloat16), 0, 1).reshape(2, 1, slots, order)
-        return jnp.where(here, x, 0).reshape(4 * slots, order)
-
-    om = jnp.where(here[0, :, :, 0], slot_omega[None, :], 0.0).reshape(2 * slots, 1)
-    om = jnp.broadcast_to(om, (2 * slots, 128))
     f32, bf16 = jnp.float32, jnp.bfloat16
     steps = 2 * ITERS
     half = 2 * seg
     dma = pltpu.SemaphoreType.DMA
     vmem = pl.BlockSpec(memory_space=pltpu.VMEM)
     hbm = pl.BlockSpec(memory_space=pl.ANY)
+    smem = pl.BlockSpec(memory_space=pltpu.SMEM)
     grad_factor = (DE_SUB / (2 * slots * order)) ** 0.5
     sizes = (n_x, n_y, face_len, float(n_x * n_y * 2 * order), grad_factor)
     sol, grad, level = pl.pallas_call(
@@ -514,7 +539,7 @@
             jax.ShapeDtypeStruct((16, 128), f32),
             jax.ShapeDtypeStruct((8, 128), f32),
         ),
-        in_specs=[vmem, vmem, vmem, vmem, hbm, hbm],
+        in_specs=[vmem, vmem, smem, smem, vmem, hbm, hbm],
         out_specs=(vmem, vmem, vmem),
         scratch_shapes=[
             pltpu.VMEM((2, 8, seg, half * 2), bf16),
@@ -530,9 +555,11 @@
             pltpu.VMEM((2, 8, 128), f32),
             pltpu.VMEM((ITERS, n_y, 24, 128), f32),
             pltpu.VMEM((ITERS, n_x, 24, 128), f32),
-            pltpu.VMEM((16, order), bf16),
-            pltpu.VMEM((16, order), bf16),
-            pltpu.VMEM((16, order), bf16),
+            pltpu.VMEM((16, order), f32),
+            pltpu.VMEM((16, order), f32),
+            pltpu.VMEM((16, order), f32),
+            pltpu.VMEM((16, order), f32),
+            pltpu.VMEM((8, 128), f32),
             pltpu.VMEM((8, 128), f32),
             pltpu.VMEM((8, 128), f32),
             dma((2, 8)), dma((3,)), dma((3,)),
@@ -543,7 +570,7 @@
         compiler_params=pltpu.CompilerParams(
             collective_id=0, has_side_effects=True, vmem_limit_bytes=50 * 1024 * 1024
         ),
-    )(all_rows(adjoint_load), all_rows(forward_state), om, owner_index[0, 0],
+    )(adjoint_load[0, 0], forward_state[0, 0], omega_table, assignment, owner_index[0, 0],
       stiffness[0, 0], mass_matrix[0, 0])
     sol = sol.reshape(2, 2, slots, 4, face_len)
     sol = lax.dynamic_index_in_dim(sol, f, axis=1, keepdims=False)

time: 96.2 us -> 92.2 us (0.958)
  Pallas kernels: 89.2 us -> 85.5 us
  other arithmetic: 1.93 us -> 0 us
  local copies, waits for them, and re-layouts: 4.07 us -> 5.74 us
    pallas_call x1, Pallas kernels: 89.2 us -> 85.5 us  [fused_body(): pl.pallas_call(functools.partial(fused_kernel, sizes), out_shape=(jax.Sha...]
    unnamed x2 -> x10, local copies, waits for them, and re-layouts: 0.71 us -> 3.7 us
    broadcast_in_dim x11 -> x0, local copies, waits for them, and re-layouts: 1.24 us -> none  [the longest x10 1.16 us: all_rows(): return jnp.where(here, x, 0).reshape(4 * slots, order)]
where the time goes in v4:
time: 92.2 us; the launch traced here: 91.9 us
  Pallas kernels  85.5 us (93%)
  local copies, waits for them, and re-layouts  5.74 us (6%)
    pallas_call x1, Pallas kernels, fused_body(): pl.pallas_call(functools.partial(fused_kernel, sizes), out_shape=(jax.Sha...  85.5 us
    unnamed x10, local copies, waits for them, and re-layouts  3.7 us

profile of v4, /device:TPU:0, one launch (start us, length us, event | category | flops | bytes accessed | tf_op | source)
XLA Modules:
  0.0 91.9 jit_solution(17698781207319524436)
XLA Ops:
  0.6 0.0 copy-start
  0.6 0.9 copy-done
  1.5 0.0 copy-start.1
  1.5 0.8 copy-done.1
  2.3 0.0 copy-start.2
  2.3 0.7 copy-done.2
  3.0 0.0 copy-start.3
  3.0 0.7 copy-done.3
  3.7 0.0 copy-start.4
  3.7 0.7 copy-done.4
  4.3 85.5 %shard_map.94 = (f32[16,3072]{1,0:T(8,128)S(1)}, f32[16,128]{1,0:T(8,128)S(1)}, f32[8,128]{1,0:T(8,128)S(1)}) custom-call(f32[4,2,4,768]{3,2,1,0:T(4,128)S(1)} %bitcast.13, bf16[4,2,4,768]{3,2,1,0:T(4,128)(2,1)S(1)} %bitcast.14, f32[8]{0:T(128)S(1)} %copy-done.3, s32[4]{0:T(128)S(1)} %copy-done.4, s32[4,768]{1,0:T(4,128)S(1)} %bitcast.15, ...), custom_call_target="tpu_custom_call" | custom-call | tf_op jit(solution)/shard_map/pallas_call | solution.py:535
  89.9 0.1 dynamic_slice.13
  90.0 0.6 broadcast_in_dim.7
  90.5 0.6 dynamic-slice_reduce_fusion
  91.2 0.1 reshape.13
  91.3 0.7 copy_bitcast_fusion
Async XLA Ops:
  0.6 0.9 copy-start
  1.5 0.8 copy-start.1
  2.3 0.7 copy-start.2
  3.0 0.7 copy-start.3
  3.7 0.7 copy-start.4
